TPU v7x, 32 devices: a whole 2x2x4 slice. The times are simulated.
32 devices in a mesh: ctx: 8 (over y, x, core), fsdp: 4 (over z).
Axes of the slice: x: 2, y: 2, z: 4, core: 2. Of those that a mesh axis runs over, the one named last changes fastest.
Arguments:
- inputs: bfloat16 [4, 1024, 2048], P('fsdp', 'ctx'), may hold values from -6 to 6
- out_grad: bfloat16 [4, 1024, 2048], P('fsdp', 'ctx'), may hold values from -6 to 6
- doc_ids: int32 [4, 1024], P('fsdp'), may hold values from 0 to 2, as said below
- block_pairs: int32 [8, 2], replicated, may hold values from 0 to 15, as said below
- qkv_weight: float32 [2048, 6144], P(('ctx', 'fsdp')), may hold values from -0.125 to 0.125
- proj_weight: float32 [2048, 2048], P(('ctx', 'fsdp')), may hold values from -1.5 to 1.5
- ffn_in_weight: float32 [2048, 11264], P(('ctx', 'fsdp')), may hold values from -0.125 to 0.125
- ffn_out_weight: float32 [5632, 2048], P(('ctx', 'fsdp')), may hold values from -0.078125 to 0.078125
- small_params: float32 [7, 2048], P(None, ('ctx', 'fsdp')), may hold values from -0.9 to 1.4, as said below
- qkv_first: float32 [2048, 6144], P(('ctx', 'fsdp')), may hold values from -40 to 40
- proj_first: float32 [2048, 2048], P(('ctx', 'fsdp')), may hold values from -4 to 4
- ffn_in_first: float32 [2048, 11264], P(('ctx', 'fsdp')), may hold values from -14 to 14
- ffn_out_first: float32 [5632, 2048], P(('ctx', 'fsdp')), may hold values from -24 to 24
- small_first: float32 [7, 2048], P(None, ('ctx', 'fsdp')), may hold values from -64 to 64
- qkv_second: float32 [2048, 6144], P(('ctx', 'fsdp')), may hold values from 217.088 to 860.16
- proj_second: float32 [2048, 2048], P(('ctx', 'fsdp')), may hold values from 1.68 to 6.72
- ffn_in_second: float32 [2048, 11264], P(('ctx', 'fsdp')), may hold values from 23.7568 to 94.208
- ffn_out_second: float32 [5632, 2048], P(('ctx', 'fsdp')), may hold values from 77.824 to 311.296
- small_second: float32 [7, 2048], P(None, ('ctx', 'fsdp')), may hold values from 614.4 to 2457.6
Outputs:
- layer_out: bfloat16 [4, 1024, 2048], P('fsdp', 'ctx')
- input_grad: bfloat16 [4, 1024, 2048], P('fsdp', 'ctx')
- qkv_weight_new: float32 [2048, 6144], P(('ctx', 'fsdp'))
- proj_weight_new: float32 [2048, 2048], P(('ctx', 'fsdp'))
- ffn_in_weight_new: float32 [2048, 11264], P(('ctx', 'fsdp'))
- ffn_out_weight_new: float32 [5632, 2048], P(('ctx', 'fsdp'))
- small_params_new: float32 [7, 2048], P(None, ('ctx', 'fsdp'))
- qkv_first_new: float32 [2048, 6144], P(('ctx', 'fsdp'))
- proj_first_new: float32 [2048, 2048], P(('ctx', 'fsdp'))
- ffn_in_first_new: float32 [2048, 11264], P(('ctx', 'fsdp'))
- ffn_out_first_new: float32 [5632, 2048], P(('ctx', 'fsdp'))
- small_first_new: float32 [7, 2048], P(None, ('ctx', 'fsdp'))
- qkv_second_new: float32 [2048, 6144], P(('ctx', 'fsdp'))
- proj_second_new: float32 [2048, 2048], P(('ctx', 'fsdp'))
- ffn_in_second_new: float32 [2048, 11264], P(('ctx', 'fsdp'))
- ffn_out_second_new: float32 [5632, 2048], P(('ctx', 'fsdp'))
- small_second_new: float32 [7, 2048], P(None, ('ctx', 'fsdp'))
- small_grads: float32 [7, 2048], P(None, ('ctx', 'fsdp'))
Inputs may be any that keep to these rules, and one draw needn't show every extreme that they name: `doc_ids`: each row of ids never falls and holds all three documents; the first and the last document each hold 128 to 256 positions. `block_pairs`: every half-block of positions is named exactly once; the two numbers of a row add up to 15. `small_params`: rows 0 and 2 lie in 0.6 to 1.4; the other rows are biases.
All inputs are finite; a program needn't handle non-finite values.
Results may differ from a plain program's by a relative error of at most 0.017.
Values may be sent and summed in bfloat16 or wider, within the bound.
A program may use at most 512 MiB of HBM per device.

v0:
```python
import functools
import math

import jax
import jax.numpy as jnp
from jax import lax
from jax.experimental import pallas as pl
from jax.experimental.pallas import tpu as pltpu
from jax.sharding import Mesh, PartitionSpec as P

D = 2048
HEADS = 32
HEAD_DIM = 64
FF = 5632
ROT = 16
STEP = 10


norm_eps = 1e-05
beta_first = 0.9
beta_second = 0.95
adam_eps = 1e-08
matrix_decay = 0.1
small_rate = 0.5


def norm_rows(values, gain_row, shift_row):
    center_mean = jnp.mean(values, axis=-1, keepdims=True)
    centered = values - center_mean
    inv_std = lax.rsqrt(jnp.mean(centered * centered, axis=-1, keepdims=True) + norm_eps)
    normed = centered * inv_std
    return (normed * gain_row + shift_row, normed, inv_std)


def norm_back(grad_rows, normed, inv_std, gain_row):
    scaled = grad_rows * gain_row
    return inv_std * (
        scaled
        - jnp.mean(scaled, axis=-1, keepdims=True)
        - normed * jnp.mean(scaled * normed, axis=-1, keepdims=True)
    )


def cross_dot(left_mat, right_mat):
    return lax.dot_general(
        left_mat, right_mat, (((0,), (0,)), ((), ())), preferred_element_type=jnp.float32
    )


def back_dot(left_mat, weight):
    return lax.dot_general(
        left_mat, weight, (((1,), (1,)), ((), ())), preferred_element_type=jnp.float32
    )


def adam_update(weight, first_moment, second_moment, gradient, step_rate, decay_factor):
    new_first = beta_first * first_moment + (1.0 - beta_first) * gradient
    new_second = beta_second * second_moment + (1.0 - beta_second) * gradient * gradient
    correct_first = 1.0 - beta_first**STEP
    correct_second = 1.0 - beta_second**STEP
    update = new_first / correct_first / (jnp.sqrt(new_second / correct_second) + adam_eps)
    return (weight - step_rate * (update + decay_factor * weight), new_first, new_second)


ROW = ("cu", "cl")
FFN_GROUP = ("cl", "fsdp")
EVERY = ("cu", "cl", "fsdp")
SCALE = HEAD_DIM**-0.5


LANES = 128


def fill_table(table, positions, start, rows):
    half_rot = ROT // 2
    here = pl.ds(pl.multiple_of(start, rows), rows)
    lane = lax.rem(lax.broadcasted_iota(jnp.int32, (1, LANES), 1), HEAD_DIM)
    inverse = jnp.zeros((1, LANES), jnp.float32)
    for i in range(half_rot):
        inverse = jnp.where(lax.rem(lane, half_rot) == i, 10000.0 ** (-2.0 * i / ROT), inverse)
    angles = positions[here, :].astype(jnp.float32) * jnp.where(lane < ROT, inverse, 0.0)
    sine = jnp.sin(angles)
    table[here, 0:LANES] = jnp.cos(angles)
    table[here, LANES : 2 * LANES] = jnp.where(lane < half_rot, -sine, 0.0)
    table[here, 2 * LANES : 3 * LANES] = jnp.where(lane < half_rot, 0.0, sine)


def turn(values, table, sign):
    keep, lower, upper = (table[:, i * LANES : (i + 1) * LANES] for i in range(3))
    half_rot = ROT // 2
    shifted = pltpu.roll(values, LANES - half_rot, 1) * lower + pltpu.roll(values, half_rot, 1) * upper
    return values * keep + sign * shifted


def dot_t(left, right):
    return lax.dot_general(left, right, (((1,), (1,)), ((), ())), preferred_element_type=jnp.float32)


def row_block(rows):
    return min(256, rows)


def project_kernel(x_ref, params_ref, w_ref, bias_ref, table_ref, normed_ref, qkv_ref):
    normed = norm_rows(x_ref[...].astype(jnp.float32), params_ref[0:1], params_ref[1:2])[0].astype(jnp.bfloat16)
    normed_ref[...] = normed
    joined = jnp.dot(normed, w_ref[...], preferred_element_type=jnp.float32) + bias_ref[...]
    turned = 2 * (joined.shape[1] // 3)
    for start in range(0, turned, LANES):
        cols = slice(start, start + LANES)
        qkv_ref[:, cols] = turn(joined[:, cols], table_ref[...], 1.0).astype(jnp.bfloat16)
    qkv_ref[:, turned:] = joined[:, turned:].astype(jnp.bfloat16)


def project(x, params, weight, bias, table):
    rows, width = x.shape
    block = row_block(rows)
    cols = weight.shape[1]

    def by_row(n):
        return pl.BlockSpec((block, n), lambda i: (i, 0))

    def whole(array):
        return pl.BlockSpec(array.shape, lambda i: (0, 0))

    return pl.pallas_call(
        project_kernel,
        grid=(rows // block,),
        in_specs=[by_row(width), whole(params), whole(weight), whole(bias), by_row(table.shape[1])],
        out_specs=[by_row(width), by_row(cols)],
        out_shape=[jax.ShapeDtypeStruct((rows, width), jnp.bfloat16), jax.ShapeDtypeStruct((rows, cols), jnp.bfloat16)],
        cost_estimate=pl.CostEstimate(
            flops=2 * rows * width * cols, bytes_accessed=4 * rows * width, transcendentals=0
        ),
        compiler_params=pltpu.CompilerParams(vmem_limit_bytes=48 << 20),
    )(x, params, weight, bias, table)


def attend_kernel(
    heads, q_ref, qkv_ref, proj_ref, pq_ref, dq_ref, pk_ref, dk_ref, mixed_ref, low_ref, tot_ref, branch_ref
):
    width = heads * HEAD_DIM
    allowed = (pk_ref[...] <= pq_ref[...]) & (dk_ref[...] == dq_ref[...])
    for head in range(heads):
        cols, key, value = (slice(p * width + head * HEAD_DIM, p * width + (head + 1) * HEAD_DIM) for p in range(3))
        scores = dot_t(q_ref[:, cols], qkv_ref[:, key]) * SCALE
        weights = jnp.where(allowed, jnp.exp(scores), 0.0)
        total = jnp.sum(weights, axis=1, keepdims=True)
        weighted = jnp.dot(weights.astype(jnp.bfloat16), qkv_ref[:, value], preferred_element_type=jnp.float32)
        mixed = weighted / total
        mixed_ref[:, cols] = mixed
        low_ref[:, cols] = mixed.astype(jnp.bfloat16)
        tot_ref[:, head : head + 1] = total
    branch_ref[...] = jnp.dot(low_ref[...], proj_ref[...], preferred_element_type=jnp.float32).astype(jnp.bfloat16)


def attend(qkv, proj, marks, heads):
    pos_col, doc_col, pos_row, doc_row = marks
    rows, cols = qkv.shape
    width = cols // 3
    block = row_block(rows)

    def by_row(n):
        return pl.BlockSpec((block, n), lambda i: (i, 0))

    def whole(array):
        return pl.BlockSpec(array.shape, lambda i: (0, 0))

    return pl.pallas_call(
        functools.partial(attend_kernel, heads),
        grid=(rows // block,),
        in_specs=[by_row(cols), whole(qkv), whole(proj), by_row(1), by_row(1), whole(pos_row), whole(doc_row)],
        out_specs=[by_row(width), by_row(width), by_row(heads), by_row(D)],
        out_shape=[
            jax.ShapeDtypeStruct((rows, width), jnp.float32),
            jax.ShapeDtypeStruct((rows, width), jnp.bfloat16),
            jax.ShapeDtypeStruct((rows, heads), jnp.float32),
            jax.ShapeDtypeStruct((rows, D), jnp.bfloat16),
        ],
        cost_estimate=pl.CostEstimate(
            flops=4 * rows * rows * width, bytes_accessed=8 * rows * D, transcendentals=rows * rows * heads
        ),
        compiler_params=pltpu.CompilerParams(vmem_limit_bytes=48 << 20),
    )(qkv, qkv, proj, pos_col, doc_col, pos_row, doc_row)


def attend_back_kernel(
    heads, qkv_ref, branch_ref, proj_ref, mixed_ref, tot_ref, pq_ref, dq_ref, pk_ref, dk_ref, table_ref, cut,
    joined_ref, bias_ref, pieces, gq_ref, gk_ref, gv_ref, own, send, recv,
):
    width = heads * HEAD_DIM
    rows = qkv_ref.shape[0]
    block = row_block(rows)
    group = cut.shape[0]

    def exchange(m):
        device, after, _, me = in_group(m)
        return Transfer(cut.at[after], pieces.at[me], send.at[m], recv.at[m], device)

    def landed(m):
        device, _, before, _ = in_group(m)
        return Transfer(cut.at[before], pieces.at[before], send.at[m], recv.at[m], device)

    me = in_group(0)[3]
    kept = pltpu.make_async_copy(cut.at[me], pieces.at[me], own.at[0])
    kept.start()
    greet_group()
    loop(1, group, lambda m: exchange(m).start())
    gk_ref[...] = jnp.zeros_like(gk_ref)
    gv_ref[...] = jnp.zeros_like(gv_ref)

    def one(step):
        here = pl.ds(pl.multiple_of(step * block, block), block)
        grad_all = dot_t(branch_ref[here], proj_ref[...])
        allowed = (pk_ref[...] <= pq_ref[here]) & (dk_ref[...] == dq_ref[here])
        for head in range(heads):
            cols, key, value = (
                slice(p * width + head * HEAD_DIM, p * width + (head + 1) * HEAD_DIM) for p in range(3)
            )
            q, k, v = qkv_ref[here, cols], qkv_ref[:, key], qkv_ref[:, value]
            inverse = 1.0 / tot_ref[here, head : head + 1]
            grad_mixed = grad_all[:, cols]
            grad_weighted = (grad_mixed * inverse).astype(jnp.bfloat16)
            grad_total = -jnp.sum(grad_mixed * mixed_ref[here, cols], axis=1, keepdims=True) * inverse
            weights = jnp.where(allowed, jnp.exp(dot_t(q, k) * SCALE), 0.0)
            grad_scores = (weights * (dot_t(grad_weighted, v) + grad_total)).astype(jnp.bfloat16)
            gq_ref[here, cols] = jnp.dot(grad_scores, k, preferred_element_type=jnp.float32) * SCALE
            gk_ref[:, cols] += cross_dot(grad_scores, q) * SCALE
            gv_ref[:, cols] += cross_dot(weights.astype(jnp.bfloat16), grad_weighted)

    loop(0, rows // block, one)
    for part, ref in enumerate((gq_ref, gk_ref, gv_ref)):
        for start in range(0, width, LANES):
            cols = slice(start, min(start + LANES, width))
            grad = ref[:, cols]
            if part < 2:
                lanes = cols.stop - cols.start
                if lanes < LANES:
                    grad = jnp.concatenate([grad, jnp.zeros((rows, LANES - lanes), jnp.float32)], axis=1)
                grad = turn(grad, table_ref[...], -1.0)[:, :lanes]
            grad = grad.astype(jnp.bfloat16)
            into = slice(part * width + cols.start, part * width + cols.stop)
            joined_ref[:, into] = grad
            bias_ref[:, into] = jnp.sum(grad.astype(jnp.float32), axis=0, keepdims=True)
    loop(1, group, lambda m: landed(m).wait_recv())
    loop(1, group, lambda m: exchange(m).wait_send())
    kept.wait()


def attend_back(qkv, grad_branch, proj, mixed, totals, marks, table, cut, heads):
    rows, cols = qkv.shape
    width = cols // 3
    return pl.pallas_call(
        functools.partial(attend_back_kernel, heads),
        in_specs=[*[VMEM] * 10, ANY],
        out_specs=[VMEM, VMEM, ANY],
        out_shape=[
            jax.ShapeDtypeStruct((rows, cols), jnp.bfloat16), jax.ShapeDtypeStruct((1, cols), jnp.float32),
            jax.ShapeDtypeStruct(cut.shape, BF16),
        ],
        scratch_shapes=[
            *[pltpu.VMEM((rows, width), jnp.float32)] * 3, DMA((1,)), DMA((cut.shape[0],)), DMA((cut.shape[0],)),
        ],
        cost_estimate=pl.CostEstimate(
            flops=10 * rows * rows * width, bytes_accessed=8 * rows * D, transcendentals=rows * rows * heads
        ),
        compiler_params=pltpu.CompilerParams(collective_id=4, has_side_effects=True, vmem_limit_bytes=60 << 20),
    )(qkv, grad_branch, proj, mixed, totals, *marks, table, cut)


def feed_kernel(x_ref, grad_ref, in_ref, out_ref, inner_ref, back_ref, in_grad_ref, x_all, back_all):
    step = pl.program_id(0)
    block = x_ref.shape[0]
    here = pl.ds(pl.multiple_of(step * block, block), block)
    hidden = out_ref.shape[0]
    gate_up = jnp.dot(x_ref[...], in_ref[...], preferred_element_type=jnp.float32)
    gate, up = gate_up[:, :hidden], gate_up[:, hidden:]
    grad_inner = dot_t(grad_ref[...], out_ref[...])
    sigmoid = 1.0 / (1.0 + jnp.exp(-gate))
    silu = gate * sigmoid
    inner_ref[...] = (silu * up).astype(jnp.bfloat16)
    grad_gate = grad_inner * up * (sigmoid * (1.0 + gate * (1.0 - sigmoid)))
    back = jnp.concatenate([grad_gate, grad_inner * silu], axis=1).astype(jnp.bfloat16)
    back_ref[...] = back
    x_all[here] = x_ref[...]
    back_all[here] = back

    @pl.when(step == x_all.shape[0] // block - 1)
    def _():
        tile = 256

        def one(i, carry):
            rows = pl.ds(pl.multiple_of(i * tile, tile), tile)
            in_grad_ref[rows] = cross_dot(x_all[:, rows], back_all[...]).astype(jnp.bfloat16)
            return carry

        lax.fori_loop(0, x_all.shape[1] // tile, one, 0)


def feed(x, grad, in_weight, out_weight):
    rows, width = x.shape
    hidden = out_weight.shape[0]
    block = row_block(rows)

    def by_row(n):
        return pl.BlockSpec((block, n), lambda i: (i, 0))

    def whole(array):
        return pl.BlockSpec(array.shape, lambda i: (0, 0))

    return pl.pallas_call(
        feed_kernel,
        grid=(rows // block,),
        in_specs=[by_row(width), by_row(width), whole(in_weight), whole(out_weight)],
        out_specs=[by_row(hidden), by_row(2 * hidden), whole(in_weight)],
        out_shape=[
            jax.ShapeDtypeStruct((rows, hidden), jnp.bfloat16), jax.ShapeDtypeStruct((rows, 2 * hidden), jnp.bfloat16),
            jax.ShapeDtypeStruct(in_weight.shape, jnp.bfloat16),
        ],
        scratch_shapes=[pltpu.VMEM((rows, width), jnp.bfloat16), pltpu.VMEM((rows, 2 * hidden), jnp.bfloat16)],
        cost_estimate=pl.CostEstimate(
            flops=10 * rows * width * hidden, bytes_accessed=8 * rows * width, transcendentals=rows * hidden
        ),
        compiler_params=pltpu.CompilerParams(vmem_limit_bytes=60 << 20),
    )(x, grad, in_weight, out_weight)


def adam_kernel(rates, chunks, *refs):
    sources, results, held = refs[:16], refs[16:28], refs[28:44]
    came, left = refs[44:]

    def rows_of(k, i):
        size = held[4 * k].shape[0] // chunks[k]
        return pl.ds(pl.multiple_of(i * size, size), size)

    def load(k, i, part):
        here = rows_of(k, i)
        at = (slice(None), here) if held[4 * k + part].ndim == 3 else (here,)
        return pltpu.make_async_copy(
            sources[4 * k + part].at[at], held[4 * k + part].at[at], came.at[4 * k + part, i]
        )

    def store(k, i, part):
        here = rows_of(k, i)
        return pltpu.make_async_copy(
            held[4 * k + part].at[here], results[3 * k + part].at[here], left.at[3 * k + part, i]
        )

    def run(k, step):
        def one(i, carry):
            step(i)
            return carry

        lax.fori_loop(0, chunks[k], one, 0)

    def start(k):
        def one(i):
            for part in range(4):
                load(k, i, part).start()

        run(k, one)

    def update(k):
        w, m, v, g = held[4 * k : 4 * k + 4]

        def one(i):
            here = rows_of(k, i)
            for part in range(4):
                load(k, i, part).wait()
            cols, parts = w.shape[1], 1
            if g.ndim == 3:
                parts = 3 if k == 1 else cols // g.shape[2]
                cols = cols // parts
            for part in range(parts):
                there = slice(part * cols, (part + 1) * cols)
                if g.ndim == 3:
                    width = g.shape[2] // parts
                    grad = jnp.concatenate(
                        [g[owner, here, part * width : (part + 1) * width] for owner in range(g.shape[0])], axis=1
                    )
                else:
                    grad = g[here, there]
                new = adam_update(
                    w[here, there], m[here, there], v[here, there], grad.astype(jnp.float32), rates[k], matrix_decay
                )
                for ref, value in zip((w, m, v), new):
                    ref[here, there] = value
            for part in range(3):
                store(k, i, part).start()

        run(k, one)

    def finish(k):
        def one(i):
            for part in range(3):
                store(k, i, part).wait()

        run(k, one)

    order = (2, 3, 0, 1)
    for k in order:
        start(k)
    for k in order:
        update(k)
    for k in order:
        finish(k)


def adam_all(states, rates):
    chunks, operands, out_shape = [], [], []
    for state in states:
        rows = state[0].shape[0]
        size = 32 if rows % 32 == 0 else 16
        chunks.append(rows // size if rows % size == 0 else 1)
        operands += state
        out_shape += [jax.ShapeDtypeStruct(state[0].shape, jnp.float32)] * 3
    any_ref = pl.BlockSpec(memory_space=pl.ANY)
    out = pl.pallas_call(
        functools.partial(adam_kernel, rates, chunks),
        in_specs=[any_ref] * 16,
        out_specs=[any_ref] * 12,
        out_shape=out_shape,
        scratch_shapes=[
            *[pltpu.VMEM(array.shape, array.dtype) for array in operands],
            pltpu.SemaphoreType.DMA((16, max(chunks))), pltpu.SemaphoreType.DMA((12, max(chunks))),
        ],
        compiler_params=pltpu.CompilerParams(vmem_limit_bytes=60 << 20),
    )(*operands)
    return [tuple(out[3 * k : 3 * k + 3]) for k in range(4)]


MESH = pl.DeviceIdType.MESH
ANY = pl.BlockSpec(memory_space=pl.ANY)
VMEM = pl.BlockSpec(memory_space=pltpu.VMEM)
DMA = pltpu.SemaphoreType.DMA
BF16, F32 = jnp.bfloat16, jnp.float32


class Transfer:
    def __init__(self, src, dst, send, recv, device):
        self.parts = (src, dst, send, recv, device)

    def copy(self):
        src, dst, send, recv, device = self.parts
        return pltpu.make_async_remote_copy(
            src_ref=src, dst_ref=dst, send_sem=send, recv_sem=recv, device_id=device, device_id_type=MESH
        )

    def start(self):
        self.copy().start()

    def wait_recv(self):
        self.copy().wait_recv()

    def wait_send(self):
        self.copy().wait_send()

    def wait(self):
        self.copy().wait()


rcopy = Transfer


def flip(index, mask):
    bit = 1
    while bit <= mask:
        if mask & bit:
            index = index + bit * (1 - 2 * lax.rem(index // bit, 2))
        bit *= 2
    return index


def place():
    return lax.axis_index("cu"), lax.axis_index("cl"), lax.axis_index("fsdp")


def sizes():
    return lax.axis_size("cu"), lax.axis_size("cl"), lax.axis_size("fsdp")


def in_group(m):
    u, c, z = place()
    _, cl, zs = sizes()
    group, me = cl * zs, c * zs + z
    after, before = lax.rem(me + m, group), lax.rem(me - m + group, group)
    return (u, after // zs, lax.rem(after, zs)), after, before, me


def greet_group():
    _, cl, zs = sizes()
    barrier = pltpu.get_barrier_semaphore()

    def signal(m, carry):
        pl.semaphore_signal(barrier, inc=1, device_id=in_group(m)[0], device_id_type=MESH)
        return carry

    lax.fori_loop(1, cl * zs, signal, 0)
    pl.semaphore_wait(barrier, cl * zs - 1)


def greet(row, line, twins=False):
    u, c, z = place()
    cu, cl, zs = sizes()
    n, me = cu * cl, u * cl + c
    barrier = pltpu.get_barrier_semaphore()

    def signal_row(m, carry):
        other = lax.rem(me + m, n)
        pl.semaphore_signal(barrier, inc=1, device_id=(other // cl, lax.rem(other, cl), z), device_id_type=MESH)
        return carry

    def signal_line(m, carry):
        pl.semaphore_signal(barrier, inc=1, device_id=(u, c, lax.rem(z + m, zs)), device_id_type=MESH)
        return carry

    def signal_twins(m, carry):
        pl.semaphore_signal(barrier, inc=1, device_id=(u, 1 - c, lax.rem(z + m, zs)), device_id_type=MESH)
        return carry

    if row:
        lax.fori_loop(1, n, signal_row, 0)
    if line:
        lax.fori_loop(1, zs, signal_line, 0)
    if twins:
        lax.fori_loop(1, zs, signal_twins, 0)
    pl.semaphore_wait(barrier, row * (n - 1) + (line + twins) * (zs - 1))


def head_kernel(
    x, small_in, qkv_far, ffn_far, proj_far, pairs, docs_in, row, par, wq, wp, in_cut, pos_col, doc_col, pos_row, doc_row,
    table, qkv_in, ffn_in, proj_in, docs, fetch, qkv, proj, small, own, x_send, x_recv, s_send, s_recv, p_send, p_recv, q_send, q_recv,
    a_send, a_recv, up_send, up_recv, dn_send, dn_recv,
):
    u, c, z = place()
    cu, cl, zs = sizes()
    n, me = cu * cl, u * cl + c
    sibling = (u, 1 - c, z)
    slab, width = qkv_in.shape[0], qkv_in.shape[1] // (3 * n)
    half = docs.shape[1]
    fetches = [
        pltpu.make_async_copy(source, into, fetch.at[i])
        for i, (source, into) in enumerate(((qkv_far, qkv_in), (proj_far, proj_in), (ffn_far, ffn_in)))
    ]
    for copy in fetches:
        copy.start()
    for i in range(docs.shape[0]):
        docs[i : i + 1] = docs_in[:, i * half : (i + 1) * half]
    small[...] = jnp.zeros_like(small)
    small[: small_in.shape[0], : small_in.shape[1]] = small_in[...]
    fetches[0].wait()
    for owner in range(n):
        for part in range(3):
            start = (part * n + owner) * width
            qkv[owner, :, part * width : (part + 1) * width] = qkv_in[:, start : start + width].astype(BF16)
    mine = [
        pltpu.make_async_copy(qkv.at[me], wq.at[me, z], own.at[0]),
        pltpu.make_async_copy(x, row.at[u, c], own.at[1]),
        pltpu.make_async_copy(small, par.at[me, z], own.at[2]),
        pltpu.make_async_copy(proj, wp.at[z], own.at[3]),
    ]
    fetches[1].wait()
    proj[...] = proj_in[...].astype(BF16)
    for copy in mine:
        copy.start()
    greet(True, True)

    def exchange(m):
        other, source = lax.rem(me + m, n), lax.rem(me - m + n, n)
        out = rcopy(
            qkv.at[other], wq.at[me, z], a_send.at[m], a_recv.at[m], (other // cl, lax.rem(other, cl), z)
        )
        into = rcopy(qkv.at[other], wq.at[source, z], a_send.at[m], a_recv.at[m], sibling)
        return out, into

    def params_line(m):
        other, source = lax.rem(z + m, zs), lax.rem(z - m + zs, zs)
        return (
            rcopy(small, par.at[me, z], p_send.at[m], p_recv.at[m], (u, c, other)),
            rcopy(small, par.at[me, source], p_send.at[m], p_recv.at[m], sibling),
        )

    def params_row(m):
        other, source = lax.rem(me + m, n), lax.rem(me - m + n, n)
        return (
            rcopy(par.at[me], par.at[me], q_send.at[m], q_recv.at[m], (other // cl, lax.rem(other, cl), z)),
            rcopy(par.at[me], par.at[source], q_send.at[m], q_recv.at[m], sibling),
        )

    def x_far(i):
        out = rcopy(x, row.at[u, c], x_send.at[i], x_recv.at[i], (flip(u, i), c, z))
        into = rcopy(x, row.at[flip(u, i), c], x_send.at[i], x_recv.at[i], sibling)
        return out, into

    def x_near(i):
        part = row.at[flip(u, i), c]
        out = rcopy(part, part, s_send.at[i], s_recv.at[i], sibling)
        into = rcopy(part, row.at[flip(u, i), 1 - c], s_send.at[i], s_recv.at[i], sibling)
        return out, into

    def loop(low, high, step):
        def run(m, carry):
            step(m)
            return carry

        lax.fori_loop(low, high, run, 0)

    loop(1, n, lambda m: exchange(m)[0].start())
    loop(1, zs, lambda m: params_line(m)[0].start())
    for copy in mine:
        copy.wait()
    for i in range(1, cu):
        x_far(i)[0].start()
    x_near(0)[0].start()

    def chain(step, m):
        piece = lax.rem(me - m + n, n)
        above, below = wq.at[piece, lax.rem(z + step, zs)], wq.at[piece, lax.rem(z - step + zs, zs)]
        return (
            rcopy(below, below, up_send.at[step, m], up_recv.at[step, m], (u, c, lax.rem(z + 1, zs))),
            rcopy(above, above, dn_send.at[step, m], dn_recv.at[step, m], (u, c, lax.rem(z - 1 + zs, zs))),
        )

    def arrival(step, m):
        piece = lax.rem(me - m + n, n)
        above, below = wq.at[piece, lax.rem(z + step + 1, zs)], wq.at[piece, lax.rem(z - step - 1 + zs, zs)]
        return (
            rcopy(below, below, up_send.at[step, m], up_recv.at[step, m], sibling),
            rcopy(above, above, dn_send.at[step, m], dn_recv.at[step, m], sibling),
        )

    def chain_proj(step):
        above, below = wp.at[lax.rem(z + step, zs)], wp.at[lax.rem(z - step + zs, zs)]
        return (
            rcopy(below, below, up_send.at[step, n], up_recv.at[step, n], (u, c, lax.rem(z + 1, zs))),
            rcopy(above, above, dn_send.at[step, n], dn_recv.at[step, n], (u, c, lax.rem(z - 1 + zs, zs))),
        )

    def forward_proj(step):
        if step:

            @pl.when(z >= step)
            def _():
                chain_proj(step - 1)[0].wait_recv()

            @pl.when(z + step < zs)
            def _():
                chain_proj(step - 1)[1].wait_recv()

        if step < zs - 1:

            @pl.when((z >= step) & (z + 1 < zs))
            def _():
                chain_proj(step)[0].start()

            @pl.when((z + step < zs) & (z > 0))
            def _():
                chain_proj(step)[1].start()

    def sent_proj(step):
        @pl.when((z >= step) & (z + 1 < zs))
        def _():
            chain_proj(step)[0].wait_send()

        @pl.when((z + step < zs) & (z > 0))
        def _():
            chain_proj(step)[1].wait_send()

    def first(m):
        @pl.when(m > 0)
        def _():
            exchange(m)[1].wait_recv()

        @pl.when(z + 1 < zs)
        def _():
            chain(0, m)[0].start()

        @pl.when(z > 0)
        def _():
            chain(0, m)[1].start()

    loop(0, n, first)
    forward_proj(0)
    fetches[2].wait()
    group, units = cl * zs, ffn_in.shape[1] // (2 * n * zs)
    for part in range(2 * cu):
        for owner in range(group):
            start = (part * group + owner) * units
            in_cut[owner, :, part * units : (part + 1) * units] = ffn_in[:, start : start + units].astype(BF16)
    lane, line_of = (lax.broadcasted_iota(jnp.int32, (half, half), d) for d in (1, 0))

    def column(values):
        return jnp.sum(jnp.where(lane == line_of, values, 0), axis=1, keepdims=True)

    for slot in range(n):
        for part in range(2):
            here = slice((2 * slot + part) * half, (2 * slot + part + 1) * half)
            number = pairs[slot, part]
            positions = number * half + lax.broadcasted_iota(jnp.int32, (1, half), 1)
            documents = docs[pl.ds(number, 1), :]
            pos_row[:, here], doc_row[:, here] = positions, documents
            pos_col[here, :], doc_col[here, :] = column(positions), column(documents)
    loop(0, n, lambda i: fill_table(table, pos_col, i * 2 * half, 2 * half))
    for m in range(1, zs):
        params_line(m)[1].wait_recv()
    loop(1, n, lambda m: params_row(m)[0].start())
    for step in range(1, zs):

        def later(m, step=step):
            @pl.when(z >= step)
            def _():
                arrival(step - 1, m)[0].wait_recv()

            @pl.when((z >= step) & (z + 1 < zs))
            def _():
                chain(step, m)[0].start()

            @pl.when(z + step < zs)
            def _():
                arrival(step - 1, m)[1].wait_recv()

            @pl.when((z + step < zs) & (z > 0))
            def _():
                chain(step, m)[1].start()

        loop(0, n, later)
        forward_proj(step)
        if step == 1:
            for i in range(1, cu):
                x_far(i)[1].wait_recv()
                x_near(i)[0].start()
    loop(1, n, lambda m: params_row(m)[1].wait_recv())
    for i in range(cu):
        x_near(i)[1].wait_recv()
    loop(1, n, lambda m: exchange(m)[0].wait_send())
    loop(1, zs, lambda m: params_line(m)[0].wait_send())
    loop(1, n, lambda m: params_row(m)[0].wait_send())
    for i in range(cu):
        x_near(i)[0].wait_send()
        if i:
            x_far(i)[0].wait_send()
    for step in range(zs - 1):

        def sent(m, step=step):
            @pl.when((z >= step) & (z + 1 < zs))
            def _():
                chain(step, m)[0].wait_send()

            @pl.when((z + step < zs) & (z > 0))
            def _():
                chain(step, m)[1].wait_send()

        loop(0, n, sent)
        sent_proj(step)


def gather_head(x, small, qkv_weight, ffn_in, proj, pairs, docs):
    cu, cl, zs = sizes()
    n = cu * cl
    slab, cols = qkv_weight.shape
    cut = (n, slab, cols // n)
    pad = (8, LANES)
    rows = docs.shape[1]
    column, line = jax.ShapeDtypeStruct((rows, 1), jnp.int32), jax.ShapeDtypeStruct((1, rows), jnp.int32)
    return pl.pallas_call(
        head_kernel,
        in_specs=[ANY, VMEM, ANY, ANY, ANY, pl.BlockSpec(memory_space=pltpu.SMEM), VMEM],
        out_specs=[ANY, ANY, ANY, ANY, *[VMEM] * 6],
        out_shape=[
            jax.ShapeDtypeStruct((cu, cl, *x.shape), x.dtype),
            jax.ShapeDtypeStruct((n, zs, *pad), F32),
            jax.ShapeDtypeStruct((n, zs, *cut[1:]), BF16),
            jax.ShapeDtypeStruct((zs, *proj.shape), BF16),
            jax.ShapeDtypeStruct((cl * zs, ffn_in.shape[0], ffn_in.shape[1] // (cl * zs)), BF16),
            column, column, line, line, jax.ShapeDtypeStruct((rows, 3 * LANES), F32),
        ],
        scratch_shapes=[
            pltpu.VMEM(qkv_weight.shape, F32), pltpu.VMEM(ffn_in.shape, F32), pltpu.VMEM(proj.shape, F32),
            pltpu.VMEM((2 * n, rows // (2 * n)), jnp.int32), DMA((3,)),
            pltpu.VMEM(cut, BF16), pltpu.VMEM(proj.shape, BF16), pltpu.VMEM(pad, F32),
            DMA((4,)), DMA((cu,)), DMA((cu,)), DMA((cu,)), DMA((cu,)), DMA((zs,)), DMA((zs,)), DMA((n,)), DMA((n,)),
            DMA((n,)), DMA((n,)), *[DMA((zs, n + 1))] * 4,
        ],
        cost_estimate=pl.CostEstimate(flops=0, bytes_accessed=200 << 20, transcendentals=0),
        compiler_params=pltpu.CompilerParams(collective_id=0, has_side_effects=True, vmem_limit_bytes=48 << 20),
    )(x, small, qkv_weight, ffn_in, proj, pairs, docs)


ITEMS = 4


def loop(low, high, step):
    def run(m, carry):
        step(m)
        return carry

    lax.fori_loop(low, high, run, 0)


def bits_of(count):
    return [1 << b for b in range(count.bit_length() - 1)]


def combos(bits):
    masks = [0]
    for b in bits:
        masks = masks + [m | b for m in masks]
    return masks


def order_of(item, count):
    return bits_of(count) if item < ITEMS // 2 else bits_of(count)[::-1]


def add_low(left, right):
    return (left.astype(F32) + right.astype(F32)).astype(BF16)


class RowReduce:
    def __init__(self, parts, held, beside, came, load, sib_s, sib_r, out_s, out_r):
        self.parts, self.held, self.beside, self.came = parts, held, beside, came
        self.load, self.sib_s, self.sib_r, self.out_s, self.out_r = load, sib_s, sib_r, out_s, out_r
        self.u, self.c, self.z = place()
        self.count = sizes()[0]
        self.phases = self.count.bit_length() - 1

    def sib(self, mask):
        return Transfer(
            self.parts.at[flip(self.u, mask), 1 - self.c], self.beside.at[mask], self.sib_s.at[mask],
            self.sib_r.at[mask], (self.u, 1 - self.c, self.z),
        )

    def loading(self, mask):
        return pltpu.make_async_copy(
            self.parts.at[flip(self.u, mask), self.c], self.held.at[mask], self.load.at[mask]
        )

    def start(self):
        for mask in reversed(range(self.count)):
            self.sib(mask).start()
            self.loading(mask).start()

    def merge(self):
        for mask in reversed(range(self.count)):
            self.loading(mask).wait()
            self.sib(mask).wait_recv()
            self.held[mask] = add_low(self.held[mask], self.beside[mask])

    def steps(self, item, phase):
        order = order_of(item, self.count)
        slot = self.count - (self.count >> phase)
        for k, rest in enumerate(combos(order[phase + 1 :])):
            yield slot + k, rest, Transfer(
                self.held.at[order[phase] | rest, item], self.came.at[slot + k, item], self.out_s.at[slot + k, item],
                self.out_r.at[slot + k, item], (flip(self.u, order[phase]), self.c, self.z),
            )

    def send(self, item, phase):
        for _, _, transfer in self.steps(item, phase):
            transfer.start()

    def add(self, item, phase):
        for slot, rest, transfer in self.steps(item, phase):
            transfer.wait_recv()
            self.held[rest, item] = add_low(self.held[rest, item], self.came[slot, item])

    def total(self, item):
        ((slot, _, transfer),) = self.steps(item, self.phases - 1)
        transfer.wait_recv()
        return self.held[0, item].astype(F32) + self.came[slot, item].astype(F32)

    def drain(self):
        for mask in range(self.count):
            self.sib(mask).wait_send()
        for item in range(ITEMS):
            for phase in range(self.phases):
                for _, _, transfer in self.steps(item, phase):
                    transfer.wait_send()

    @staticmethod
    def scratch(count, rows, width):
        block = (count, ITEMS, rows // ITEMS, width)
        return [
            pltpu.VMEM(block, BF16), pltpu.VMEM(block, BF16), pltpu.VMEM(block, BF16), DMA((count,)), DMA((count,)),
            DMA((count,)), DMA((count, ITEMS)), DMA((count, ITEMS)),
        ]


class RowGather:
    def __init__(self, own, full, keep, out_s, out_r, sib_s, sib_r):
        self.own, self.full, self.keep = own, full, keep
        self.out_s, self.out_r, self.sib_s, self.sib_r = out_s, out_r, sib_s, sib_r
        self.u, self.c, self.z = place()
        self.count = sizes()[0]
        self.phases = self.count.bit_length() - 1

    def kept(self, item):
        return pltpu.make_async_copy(self.own.at[item], self.full.at[self.u, self.c, item], self.keep.at[item])

    def source(self, mask, item):
        return self.own.at[item] if mask == 0 else self.full.at[flip(self.u, mask), self.c, item]

    def sib(self, mask, item):
        return Transfer(
            self.source(mask, item), self.full.at[flip(self.u, mask), self.c, item], self.sib_s.at[mask, item],
            self.sib_r.at[mask, item], (self.u, 1 - self.c, self.z),
        )

    def steps(self, item, phase):
        order = order_of(item, self.count)
        for k, mask in enumerate(combos(order[:phase])):
            slot = (1 << phase) - 1 + k
            yield mask | order[phase], Transfer(
                self.source(mask, item), self.full.at[flip(self.u, mask), self.c, item], self.out_s.at[slot, item],
                self.out_r.at[slot, item], (flip(self.u, order[phase]), self.c, self.z),
            )

    def start(self, item):
        self.send(item, 0)
        self.sib(0, item).start()
        self.kept(item).start()

    def send(self, item, phase):
        for _, transfer in self.steps(item, phase):
            transfer.start()

    def pass_on(self, item, phase):
        for mask, transfer in self.steps(item, phase):
            transfer.wait_recv()
            self.sib(mask, item).start()

    def drain(self):
        for item in range(ITEMS):
            self.kept(item).wait()
            for mask in range(self.count):
                self.sib(mask, item).wait()
            for phase in range(self.phases):
                for _, transfer in self.steps(item, phase):
                    transfer.wait_send()

    @staticmethod
    def scratch(count):
        return [DMA((ITEMS,)), *[DMA((count, ITEMS))] * 4]


class PlaneGather:
    def __init__(self, own, full, keep, out_s, out_r):
        self.own, self.full, self.keep, self.out_s, self.out_r = own, full, keep, out_s, out_r
        self.u, self.c, self.z = place()
        self.count = sizes()[0]
        self.items = own.shape[0]
        self.phases = self.count.bit_length() - 1

    def kept(self, item):
        return pltpu.make_async_copy(self.own.at[item], self.full.at[self.u, item], self.keep.at[item])

    def steps(self, item, phase):
        order = bits_of(self.count) if item % 2 else bits_of(self.count)[::-1]
        for k, mask in enumerate(combos(order[:phase])):
            slot = (1 << phase) - 1 + k
            block = self.full.at[flip(self.u, mask), item]
            yield Transfer(
                self.own.at[item] if mask == 0 else block, block, self.out_s.at[slot, item],
                self.out_r.at[slot, item], (flip(self.u, order[phase]), self.c, self.z),
            )

    def start(self):
        for item in range(self.items):
            self.kept(item).start()
            for transfer in self.steps(item, 0):
                transfer.start()

    def step(self, phase):
        for item in range(self.items):
            for transfer in self.steps(item, phase - 1):
                transfer.wait_recv()
            if phase < self.phases:
                for transfer in self.steps(item, phase):
                    transfer.start()

    def drain(self):
        for item in range(self.items):
            self.kept(item).wait()
            for phase in range(self.phases):
                for transfer in self.steps(item, phase):
                    transfer.wait_send()

    @staticmethod
    def scratch(count, items):
        return [DMA((items,)), DMA((count, items)), DMA((count, items))]


class LineGather:
    def __init__(self, own, full, keep, up_s, up_r, dn_s, dn_r, sib_s, sib_r):
        self.own, self.full, self.keep = own, full, keep
        self.up_s, self.up_r, self.dn_s, self.dn_r, self.sib_s, self.sib_r = up_s, up_r, dn_s, dn_r, sib_s, sib_r
        self.u, self.c, self.z = place()
        self.count = sizes()[2]

    def kept(self, item):
        return pltpu.make_async_copy(self.own.at[item], self.full.at[self.z, self.c, item], self.keep.at[item])

    def up(self, item, step):
        origin = lax.rem(self.z - step + self.count, self.count)
        block = self.full.at[origin, self.c, item]
        source = self.own.at[item] if step == 0 else block
        to = lax.rem(self.z + 1, self.count)
        return Transfer(source, block, self.up_s.at[step, item], self.up_r.at[step, item], (self.u, self.c, to))

    def down(self, item, step):
        block = self.full.at[lax.rem(self.z + step, self.count), self.c, item]
        source = self.own.at[item] if step == 0 else block
        to = lax.rem(self.z - 1 + self.count, self.count)
        return Transfer(source, block, self.dn_s.at[step, item], self.dn_r.at[step, item], (self.u, self.c, to))

    def sib(self, item, origin, own=False):
        block = self.full.at[origin, self.c, item]
        return Transfer(
            self.own.at[item] if own else block, block, self.sib_s.at[origin, item], self.sib_r.at[origin, item],
            (self.u, 1 - self.c, self.z),
        )

    def start(self, item):
        @pl.when(self.z + 1 < self.count)
        def _():
            self.up(item, 0).start()

        @pl.when(self.z > 0)
        def _():
            self.down(item, 0).start()

        self.sib(item, self.z, True).start()
        self.kept(item).start()

    def forward(self, item, step):
        z, count = self.z, self.count

        @pl.when(z >= step)
        def _():
            self.up(item, step - 1).wait_recv()
            if step < count - 1:

                @pl.when(z + 1 < count)
                def _():
                    self.up(item, step).start()

            self.sib(item, z - step).start()

        @pl.when(z + step < count)
        def _():
            self.down(item, step - 1).wait_recv()
            if step < count - 1:

                @pl.when(z > 0)
                def _():
                    self.down(item, step).start()

            self.sib(item, z + step).start()

    def drain(self):
        z, count = self.z, self.count
        for item in range(ITEMS):
            self.kept(item).wait()
            for origin in range(count):
                self.sib(item, origin).wait()
            for step in range(count - 1):

                @pl.when((z >= step) & (z + 1 < count))
                def _(item=item, step=step):
                    self.up(item, step).wait_send()

                @pl.when((z + step < count) & (z > 0))
                def _(item=item, step=step):
                    self.down(item, step).wait_send()

    @staticmethod
    def scratch(count):
        return [DMA((ITEMS,)), *[DMA((count, ITEMS))] * 6]


def far_first(count, z):
    table = []
    for i in range(count):
        ends = sorted(range(count), key=lambda to: (-abs(to - i), 0 if (to > i) == (2 * i < count) else 1))
        lead = [to for to in ends if (to > i) == (2 * i < count) and to != i]
        rest = [to for to in ends if (to > i) != (2 * i < count) and to != i]
        mixed = []
        while lead or rest:
            mixed += lead[:1] + rest[:1]
            lead, rest = lead[1:], rest[1:]
        table.append(mixed + [i])
    power, term = 1, 1
    for k in range(1, count):
        term = (term * (z - k + 1) * (count - 1)) // k
        power = power + term
    packed = [sum(table[i][k] * count**i for i in range(count)) for k in range(count)]
    return [lax.rem(p // power, count) for p in packed]


class LineReduce:
    def __init__(self, held, from_below, from_above, pieces, up_s, up_r, dn_s, dn_r):
        self.held, self.from_below, self.from_above, self.pieces = held, from_below, from_above, pieces
        self.up_s, self.up_r, self.dn_s, self.dn_r = up_s, up_r, dn_s, dn_r
        self.u, self.c, self.z = place()
        self.count = sizes()[2]

    def up(self, to, piece):
        return Transfer(
            self.held.at[to, piece], self.from_below.at[to, piece], self.up_s.at[to, piece], self.up_r.at[to, piece],
            (self.u, self.c, lax.rem(self.z + 1, self.count)),
        )

    def down(self, to, piece):
        return Transfer(
            self.held.at[to, piece], self.from_above.at[to, piece], self.dn_s.at[to, piece], self.dn_r.at[to, piece],
            (self.u, self.c, lax.rem(self.z - 1 + self.count, self.count)),
        )

    def step(self, t):
        z, count = self.z, self.count
        far_up, far_down = count - 1 - t, t

        def upward(piece):
            @pl.when(z > 0)
            def _():
                self.up(far_up, piece).wait_recv()
                self.held[far_up, piece] = add_low(self.held[far_up, piece], self.from_below[far_up, piece])

            self.up(far_up, piece).start()

        def downward(piece):
            @pl.when(z < count - 1)
            def _():
                self.down(far_down, piece).wait_recv()
                self.held[far_down, piece] = add_low(self.held[far_down, piece], self.from_above[far_down, piece])

            self.down(far_down, piece).start()

        lag = min(3, self.pieces // 2)
        late_up = lag * ((2 * z) // count)

        def one(i):
            piece_up, piece_down = i - late_up, i - (lag - late_up)

            @pl.when((z < far_up) & (piece_up >= 0) & (piece_up < self.pieces))
            def _():
                upward(piece_up)

            @pl.when((z > far_down) & (piece_down >= 0) & (piece_down < self.pieces))
            def _():
                downward(piece_down)

        loop(0, self.pieces + lag, one)

    def total(self, piece, into):
        z, count = self.z, self.count
        into[...] = self.held[z, piece].astype(F32)

        @pl.when(z > 0)
        def _():
            self.up(z, piece).wait_recv()
            into[...] += self.from_below[z, piece].astype(F32)

        @pl.when(z < count - 1)
        def _():
            self.down(z, piece).wait_recv()
            into[...] += self.from_above[z, piece].astype(F32)

    def drain(self):
        z, count = self.z, self.count
        for t in range(count - 1):
            far_up, far_down = count - 1 - t, t

            def one(piece, far_up=far_up, far_down=far_down):
                @pl.when(z < far_up)
                def _():
                    self.up(far_up, piece).wait_send()

                @pl.when(z > far_down)
                def _():
                    self.down(far_down, piece).wait_send()

            loop(0, self.pieces, one)

    @staticmethod
    def scratch(count, pieces, block):
        shape = (count, pieces, *block)
        return [*[pltpu.VMEM(shape, BF16)] * 3, *[DMA((count, pieces))] * 4]


def mid_forward_kernel(branch, x, out_grad, params, cut, hidden, mlp, grads, weight, low, *scratch):
    reduce = RowReduce(branch, *scratch[:8])
    gather = LineGather(low, mlp, *scratch[8:15])
    gather_grads = LineGather(out_grad, grads, *scratch[15:22])
    plane = PlaneGather(cut, weight, *scratch[22:])
    greet(True, True)
    reduce.start()
    for item in range(ITEMS):
        gather_grads.start(item)
    reduce.merge()
    for item in range(ITEMS):
        reduce.send(item, 0)
    plane.start()
    for item in range(ITEMS):
        gather_grads.forward(item, 1)
    for phase in range(1, reduce.phases):
        for item in range(ITEMS):
            reduce.add(item, phase - 1)
            reduce.send(item, phase)
    for step in range(2, gather.count - 1):
        for item in range(ITEMS):
            gather_grads.forward(item, step)
    for item in range(ITEMS):
        state = x[item].astype(F32) + reduce.total(item)
        hidden[item] = state
        low[item] = norm_rows(state, params[0:1], params[1:2])[0].astype(BF16)
        gather.start(item)
    plane.step(1)
    for step in range(1, gather.count):
        for item in range(ITEMS):
            gather.forward(item, step)
        if step == 1:
            for item in range(ITEMS):
                gather_grads.forward(item, gather.count - 1)
    for phase in range(2, plane.phases + 1):
        plane.step(phase)
    gather_grads.drain()
    gather.drain()
    plane.drain()
    reduce.drain()


def mid_forward(branch, x, out_grad, params, cut):
    cu, cl, zs = sizes()
    rows, width = x.shape
    block = (ITEMS, rows // ITEMS, width)
    full = jax.ShapeDtypeStruct((zs, cl, *block), BF16)
    hidden, mlp, grads, weight, _ = pl.pallas_call(
        mid_forward_kernel,
        in_specs=[ANY, VMEM, VMEM, VMEM, ANY],
        out_specs=[VMEM, ANY, ANY, ANY, VMEM],
        out_shape=[
            jax.ShapeDtypeStruct(block, F32), full, full, jax.ShapeDtypeStruct((cu, *cut.shape), BF16),
            jax.ShapeDtypeStruct(block, BF16),
        ],
        scratch_shapes=[
            *RowReduce.scratch(cu, rows, width), *LineGather.scratch(zs), *LineGather.scratch(zs),
            *PlaneGather.scratch(cu, cut.shape[0]),
        ],
        cost_estimate=pl.CostEstimate(flops=0, bytes_accessed=200 << 20, transcendentals=0),
        compiler_params=pltpu.CompilerParams(collective_id=1, has_side_effects=True, vmem_limit_bytes=56 << 20),
    )(branch.reshape(cu, cl, *block), x.reshape(block), out_grad.reshape(block), params, cut)
    group_rows = cl * zs * rows
    return (
        hidden.reshape(rows, width), mlp.reshape(group_rows, width), grads.reshape(group_rows, width),
        weight.reshape(width, cut.shape[2]),
    )


def mid_backward_kernel(
    back, in_weight, hidden, out_grad, params, inner, weight, grads,
    grad_hidden, full, sums, layer_out, weight_grad, low,
    held, below, above, up_s, up_r, dn_s, dn_r, both, beside, total, sib_s, sib_r,
    held_out, below_out, above_out, up_so, up_ro, dn_so, dn_ro, both_out, beside_out, sib_so, sib_ro,
    back_v, in_weight_v, inner_v, weight_v, grads_v, fetch, *scratch,
):
    u, c, z = place()
    _, cl, zs = sizes()
    rows = ITEMS * held.shape[2]
    width = weight_v.shape[1]
    reduce = LineReduce(held, below, above, ITEMS, up_s, up_r, dn_s, dn_r)
    reduce_out = LineReduce(held_out, below_out, above_out, ITEMS, up_so, up_ro, dn_so, dn_ro)
    gather = RowGather(low, full, *scratch)
    fetches = [
        pltpu.make_async_copy(source, into, fetch.at[i])
        for i, (source, into) in enumerate(
            ((back, back_v), (in_weight, in_weight_v), (inner, inner_v), (weight, weight_v), (grads, grads_v))
        )
    ]
    for copy in fetches:
        copy.start()

    def sib(to):
        return Transfer(both.at[to, 1 - c], beside.at[to], sib_s.at[to], sib_r.at[to], (u, 1 - c, z))

    def sib_out(to):
        return Transfer(both_out.at[to, 1 - c], beside_out.at[to], sib_so.at[to], sib_ro.at[to], (u, 1 - c, z))

    tile = 512

    def multiply(to, into, left, product):
        def one(i):
            cols = pl.ds(pl.multiple_of(i * tile, tile), tile)
            here = pl.ds(pl.multiple_of(to * (cl * rows), cl * rows), cl * rows)
            part = product(left[here], cols).astype(BF16)
            into[to, :, :, :, cols] = part.reshape(cl, ITEMS, rows // ITEMS, tile)

        loop(0, width // tile, one)

    order = far_first(zs, z)
    fetches[0].wait()
    fetches[1].wait()
    multiply(order[0], both, back_v, lambda left, cols: dot_t(left, in_weight_v[cols]))
    greet(True, True)
    sib(order[0]).start()
    def settle(to):
        sib(to).wait_recv()
        held[to] = add_low(both[to, c], beside[to])

    def settle_out(to):
        sib_out(to).wait_recv()
        held_out[to] = add_low(both_out[to, c], beside_out[to])

    at_end = (z == 0) | (z == zs - 1)
    inside = jnp.logical_not(at_end)
    for k in range(1, zs):
        multiply(order[k], both, back_v, lambda left, cols: dot_t(left, in_weight_v[cols]))
        sib(order[k]).start()
        settle(order[k - 1])

        @pl.when(at_end)
        def _(t=k - 1):
            reduce.step(t)

    settle(order[zs - 1])

    @pl.when(inside)
    def _():
        reduce.step(0)

    fetches[2].wait()
    fetches[3].wait()
    for k in range(zs):
        multiply(
            order[k], both_out, inner_v,
            lambda left, cols: jnp.dot(left, weight_v[:, cols], preferred_element_type=F32),
        )
        sib_out(order[k]).start()

    @pl.when(inside)
    def _():
        for t in range(1, zs - 1):
            reduce.step(t)

    for to in order:
        settle_out(to)

    @pl.when(at_end)
    def _():
        for t in range(zs - 1):
            reduce_out.step(t)

    sums[...] = jnp.zeros_like(sums)
    for item in range(ITEMS):
        reduce.total(item, total)
        _, hat, inverse = norm_rows(hidden[item], params[0:1], params[1:2])
        grad = total[...]
        sums[0:1] += jnp.sum(grad * hat, axis=0, keepdims=True)
        sums[1:2] += jnp.sum(grad, axis=0, keepdims=True)
        grad = out_grad[item].astype(F32) + norm_back(grad, hat, inverse, params[0:1])
        grad_hidden[item] = grad
        low[item] = grad.astype(BF16)
        gather.start(item)
    fetches[4].wait()

    def outer(i):
        cols = pl.ds(pl.multiple_of(i * tile, tile), tile)
        weight_grad[:, cols] = cross_dot(inner_v[...], grads_v[:, cols]).astype(BF16)

    loop(0, width // tile, outer)
    for phase in range(gather.phases):
        for item in range(ITEMS):
            gather.pass_on(item, phase)
            if phase + 1 < gather.phases:
                gather.send(item, phase + 1)
        if phase == 0:

            @pl.when(inside)
            def _():
                reduce_out.step(0)

    @pl.when(inside)
    def _():
        for t in range(1, zs - 1):
            reduce_out.step(t)

    for item in range(ITEMS):
        reduce_out.total(item, total)
        layer_out[item] = (hidden[item] + total[...]).astype(BF16)
    gather.drain()
    reduce.drain()
    reduce_out.drain()
    for to in range(zs):
        sib(to).wait_send()
        sib_out(to).wait_send()


def mid_backward(back_rows, in_weight, hidden, out_grad, params, inner, weight, grads):
    cu, cl, zs = sizes()
    rows, width = out_grad.shape
    block = (ITEMS, rows // ITEMS, width)
    shares = pltpu.VMEM((zs, *block), BF16)
    both = pltpu.VMEM((zs, cl, *block), BF16)
    grad_hidden, full, sums, layer_out, weight_grad, _ = pl.pallas_call(
        mid_backward_kernel,
        in_specs=[ANY, ANY, VMEM, VMEM, VMEM, ANY, ANY, ANY],
        out_specs=[VMEM, ANY, VMEM, VMEM, VMEM, VMEM],
        out_shape=[
            jax.ShapeDtypeStruct(block, F32),
            jax.ShapeDtypeStruct((cu, cl, *block), BF16),
            jax.ShapeDtypeStruct((2, width), F32),
            jax.ShapeDtypeStruct(block, BF16),
            jax.ShapeDtypeStruct(weight.shape, BF16),
            jax.ShapeDtypeStruct(block, BF16),
        ],
        scratch_shapes=[
            *LineReduce.scratch(zs, ITEMS, block[1:]), both, shares, pltpu.VMEM(block[1:], F32), DMA((zs,)), DMA((zs,)),
            *LineReduce.scratch(zs, ITEMS, block[1:]), both, shares, DMA((zs,)), DMA((zs,)),
            pltpu.VMEM(back_rows.shape, BF16), pltpu.VMEM(in_weight.shape, BF16), pltpu.VMEM(inner.shape, BF16),
            pltpu.VMEM(weight.shape, BF16), pltpu.VMEM(grads.shape, BF16), DMA((5,)), *RowGather.scratch(cu),
        ],
        cost_estimate=pl.CostEstimate(flops=0, bytes_accessed=200 << 20, transcendentals=0),
        compiler_params=pltpu.CompilerParams(collective_id=2, has_side_effects=True, vmem_limit_bytes=62 << 20),
    )(back_rows, in_weight, hidden.reshape(block), out_grad.reshape(block), params, inner, weight, grads)
    return (
        grad_hidden.reshape(rows, width), full.reshape(cu * cl * rows, width), sums, layer_out.reshape(rows, width),
        weight_grad,
    )


def tail_kernel(parts, x, grad_hidden, params, terms, grads, proj, input_grad, small, cut, proj_grad, pile, line_in, row_in, total,
                row_total, line_s, line_r, row_s, row_r, a_send, a_recv, own, held_load, low, *scratch):
    u, c, z = place()
    cu, cl, zs = sizes()
    n, me = cu * cl, u * cl + c
    reduce = RowReduce(parts, *scratch[:8])
    held, held_proj = scratch[8], scratch[15]
    line = LineReduce(*scratch[8:11], n, *scratch[11:15])
    line_proj = LineReduce(*scratch[15:18], 1, *scratch[18:])
    load = pltpu.make_async_copy(grads, held, held_load.at[0])
    load_proj = pltpu.make_async_copy(proj, held_proj, held_load.at[1])
    load.start()
    load_proj.start()
    greet(True, True)
    reduce.start()
    load.wait()
    load_proj.wait()
    line.step(0)
    line_proj.step(0)
    reduce.merge()
    for item in range(ITEMS):
        reduce.send(item, 0)
    for t in range(1, zs - 1):
        line.step(t)
        line_proj.step(t)
    for phase in range(1, reduce.phases):
        for item in range(ITEMS):
            reduce.add(item, phase - 1)
            reduce.send(item, phase)
    pile[...] = terms[...]
    for item in range(ITEMS):
        grad = reduce.total(item)
        _, hat, inverse = norm_rows(x[item].astype(F32), params[0:1], params[1:2])
        pile[0:1] += jnp.sum(grad * hat, axis=0, keepdims=True)
        pile[1:2] += jnp.sum(grad, axis=0, keepdims=True)
        grad = grad_hidden[item] + norm_back(grad, hat, inverse, params[0:1])
        input_grad[item] = grad.astype(BF16)

    def along_line(m):
        return Transfer(pile, line_in.at[m], line_s.at[m], line_r.at[m], (u, c, lax.rem(z + m, zs)))

    def along_row(m):
        other = lax.rem(me + m, n)
        return Transfer(
            total, row_in.at[m], row_s.at[m], row_r.at[m], (other // cl, lax.rem(other, cl), z)
        )

    def exchange(m):
        other = lax.rem(me + m, n)
        return Transfer(
            low.at[other], cut.at[me], a_send.at[m], a_recv.at[m], (other // cl, lax.rem(other, cl), z)
        )

    def landed(m):
        source = lax.rem(me - m + n, n)
        return Transfer(
            low.at[source], cut.at[source], a_send.at[m], a_recv.at[m], (u, 1 - c, z)
        )

    loop(1, zs, lambda m: along_line(m).start())

    def finish(m):
        piece = lax.rem(me + m, n)
        line.total(piece, row_total)
        low[piece] = row_total[...].astype(BF16)

        @pl.when(m > 0)
        def _():
            exchange(m).start()

    loop(0, n, finish)
    line_proj.total(0, proj_grad)
    mine = pltpu.make_async_copy(low.at[me], cut.at[me], own.at[0])
    mine.start()
    total[...] = pile[...]
    for m in range(1, zs):
        along_line(m).wait_recv()
        total[...] += line_in[m]
    loop(1, n, lambda m: along_row(m).start())
    small[...] = total[...]

    def collect(m):
        along_row(m).wait_recv()
        small[...] += row_in[m]

    loop(1, n, collect)
    loop(1, n, lambda m: landed(m).wait_recv())
    mine.wait()
    loop(1, n, lambda m: exchange(m).wait_send())
    loop(1, n, lambda m: along_row(m).wait_send())
    loop(1, zs, lambda m: along_line(m).wait_send())
    reduce.drain()
    line.drain()
    line_proj.drain()


def tail(parts, x, grad_hidden, params, terms, grads, proj):
    cu, cl, zs = sizes()
    n = cu * cl
    rows, width = x.shape
    block = (ITEMS, rows // ITEMS, width)
    piece = grads.shape[2:]
    input_grad, small, cut, proj_grad = pl.pallas_call(
        tail_kernel,
        in_specs=[ANY, VMEM, VMEM, VMEM, VMEM, ANY, ANY],
        out_specs=[VMEM, VMEM, ANY, VMEM],
        out_shape=[
            jax.ShapeDtypeStruct(block, BF16),
            jax.ShapeDtypeStruct((8, width), F32),
            jax.ShapeDtypeStruct((n, *piece), BF16),
            jax.ShapeDtypeStruct(proj.shape[2:], F32),
        ],
        scratch_shapes=[
            pltpu.VMEM((8, width), F32), pltpu.VMEM((zs, 8, width), F32), pltpu.VMEM((n, 8, width), F32),
            pltpu.VMEM((8, width), F32), pltpu.VMEM(piece, F32), DMA((zs,)), DMA((zs,)), DMA((n,)), DMA((n,)),
            DMA((n,)), DMA((n,)), DMA((1,)), DMA((2,)), pltpu.VMEM((n, *piece), BF16),
            *RowReduce.scratch(cu, rows, width), *LineReduce.scratch(zs, n, piece),
            *LineReduce.scratch(zs, 1, proj.shape[2:]),
        ],
        cost_estimate=pl.CostEstimate(flops=0, bytes_accessed=200 << 20, transcendentals=0),
        compiler_params=pltpu.CompilerParams(collective_id=3, has_side_effects=True, vmem_limit_bytes=60 << 20),
    )(parts.reshape(cu, cl, *block), x.reshape(block), grad_hidden.reshape(block), params, terms, grads, proj)
    return input_grad.reshape(rows, width), small, cut, proj_grad


def back_kernel(
    heads, qkv_ref, low_ref, tot_ref, pq_ref, dq_ref, pk_ref, dk_ref, table_ref,
    x, grad_hidden, params, mid_sums, branch, proj, mixed, normed, weight, in_cut,
    input_grad, small, cut, proj_grad, in_pieces,
    gq_ref, gk_ref, gv_ref, joined_ref, branch_ref, proj_ref, mixed_ref, normed_v, weight_v, parts, fetch, in_s, in_r,
    pile, line_in, row_in, total, row_total, line_s, line_r, row_s, row_r, a_s, a_r, own, low, *scratch,
):
    u, c, z = place()
    cu, cl, zs = sizes()
    n, me = cu * cl, u * cl + c
    width = heads * HEAD_DIM
    rows = qkv_ref.shape[0]
    block = row_block(rows)
    slab = low.shape[1]
    group = in_cut.shape[0]
    reduce = RowReduce(parts, *scratch[:8])
    held, held_proj = scratch[8], scratch[15]
    line = LineReduce(*scratch[8:11], n, *scratch[11:15])
    line_proj = LineReduce(*scratch[15:18], 1, *scratch[18:])
    my_place = in_group(0)[3]
    kept = pltpu.make_async_copy(in_cut.at[my_place], in_pieces.at[my_place], own.at[1])
    fetches = [
        pltpu.make_async_copy(source, into, fetch.at[i])
        for i, (source, into) in enumerate(
            ((branch, branch_ref), (proj, proj_ref), (mixed, mixed_ref), (normed, normed_v), (weight, weight_v))
        )
    ]

    def in_exchange(m):
        device, after, _, mine = in_group(m)
        return Transfer(in_cut.at[after], in_pieces.at[mine], in_s.at[m], in_r.at[m], device)

    def in_landed(m):
        device, _, before, _ = in_group(m)
        return Transfer(in_cut.at[before], in_pieces.at[before], in_s.at[m], in_r.at[m], device)

    for copy in (kept, *fetches):
        copy.start()
    greet(True, True, True)
    loop(1, group, lambda m: in_exchange(m).start())
    for copy in fetches[:3]:
        copy.wait()
    tile = 512

    def proj_tile(i):
        cols = pl.ds(pl.multiple_of(i * tile, tile), tile)
        grad = cross_dot(low_ref[...], branch_ref[:, cols]).astype(BF16)
        held_proj[:, 0, :, cols] = grad.reshape(zs, slab, tile)

    loop(0, D // tile, proj_tile)
    at_end = (z == 0) | (z == zs - 1)

    @pl.when(at_end)
    def _():
        for t in range(zs - 1):
            line_proj.step(t)

    gk_ref[...] = jnp.zeros_like(gk_ref)
    gv_ref[...] = jnp.zeros_like(gv_ref)

    def one(step):
        here = pl.ds(pl.multiple_of(step * block, block), block)
        grad_all = dot_t(branch_ref[here], proj_ref[...])
        allowed = (pk_ref[...] <= pq_ref[here]) & (dk_ref[...] == dq_ref[here])
        for head in range(heads):
            cols, key, value = (
                slice(p * width + head * HEAD_DIM, p * width + (head + 1) * HEAD_DIM) for p in range(3)
            )
            q, k, v = qkv_ref[here, cols], qkv_ref[:, key], qkv_ref[:, value]
            inverse = 1.0 / tot_ref[here, head : head + 1]
            grad_mixed = grad_all[:, cols]
            grad_weighted = (grad_mixed * inverse).astype(BF16)
            grad_total = -jnp.sum(grad_mixed * mixed_ref[here, cols], axis=1, keepdims=True) * inverse
            weights = jnp.where(allowed, jnp.exp(dot_t(q, k) * SCALE), 0.0)
            grad_scores = (weights * (dot_t(grad_weighted, v) + grad_total)).astype(BF16)
            gq_ref[here, cols] = jnp.dot(grad_scores, k, preferred_element_type=F32) * SCALE
            gk_ref[:, cols] += cross_dot(grad_scores, q) * SCALE
            gv_ref[:, cols] += cross_dot(weights.astype(BF16), grad_weighted)

    blocks = rows // block
    loop(0, blocks // 2, one)

    @pl.when(jnp.logical_not(at_end))
    def _():
        line_proj.step(0)

    loop(blocks // 2, blocks, one)

    @pl.when(jnp.logical_not(at_end))
    def _():
        for t in range(1, zs - 1):
            line_proj.step(t)


    pile[...] = jnp.zeros_like(pile)
    for part, ref in enumerate((gq_ref, gk_ref, gv_ref)):
        for start in range(0, width, LANES):
            grad = ref[:, start : start + LANES]
            if part < 2:
                grad = turn(grad, table_ref[...], -1.0)
            grad = grad.astype(BF16)
            joined_ref[:, part * width + start : part * width + start + LANES] = grad
            there = pl.ds(pl.multiple_of(me * width + start, LANES), LANES)
            pile[4 + part : 5 + part, there] = jnp.sum(grad.astype(F32), axis=0, keepdims=True)
    for copy in fetches[3:]:
        copy.wait()

    def qkv_tile(i):
        cols = pl.ds(pl.multiple_of(i * zs * slab, zs * slab), zs * slab)
        grad = cross_dot(normed_v[:, cols], joined_ref[...]).astype(BF16)
        for to in range(zs):
            held[to, i] = grad[to * slab : (to + 1) * slab]

    loop(0, n, qkv_tile)

    @pl.when(at_end)
    def _():
        for t in range(zs - 1):
            line.step(t)


    def norm_tile(i):
        to, col = i // (D // tile), lax.rem(i, D // tile) * tile
        cols = pl.ds(pl.multiple_of(col, tile), tile)
        here = pl.ds(pl.multiple_of(to * (rows // cu), rows // cu), rows // cu)
        part = dot_t(joined_ref[here], weight_v[cols]).astype(BF16)
        parts[to, :, :, :, cols] = part.reshape(cl, ITEMS, rows // (n * ITEMS), tile)

    loop(0, cu * (D // tile), norm_tile)
    reduce.start()
    reduce.merge()
    for item in range(ITEMS):
        reduce.send(item, 0)

    @pl.when(jnp.logical_not(at_end))
    def _():
        line.step(0)

    for phase in range(1, reduce.phases):
        for item in range(ITEMS):
            reduce.add(item, phase - 1)
            reduce.send(item, phase)
    pile[2:4] = mid_sums[...]
    for item in range(ITEMS):
        grad = reduce.total(item)
        _, hat, inverse = norm_rows(x[item].astype(F32), params[0:1], params[1:2])
        pile[0:1] += jnp.sum(grad * hat, axis=0, keepdims=True)
        pile[1:2] += jnp.sum(grad, axis=0, keepdims=True)
        grad = grad_hidden[item] + norm_back(grad, hat, inverse, params[0:1])
        input_grad[item] = grad.astype(BF16)

    def along_line(m):
        return Transfer(pile, line_in.at[m], line_s.at[m], line_r.at[m], (u, c, lax.rem(z + m, zs)))

    def along_row(m):
        other = lax.rem(me + m, n)
        return Transfer(total, row_in.at[m], row_s.at[m], row_r.at[m], (other // cl, lax.rem(other, cl), z))

    def exchange(m):
        other = lax.rem(me + m, n)
        return Transfer(low.at[other], cut.at[me], a_s.at[m], a_r.at[m], (other // cl, lax.rem(other, cl), z))

    def landed(m):
        source = lax.rem(me - m + n, n)
        return Transfer(low.at[source], cut.at[source], a_s.at[m], a_r.at[m], (u, 1 - c, z))

    loop(1, zs, lambda m: along_line(m).start())

    @pl.when(jnp.logical_not(at_end))
    def _():
        for t in range(1, zs - 1):
            line.step(t)

    total[...] = pile[...]
    for m in range(1, zs):
        along_line(m).wait_recv()
        total[...] += line_in[m]
    loop(1, n, lambda m: along_row(m).start())

    def finish(piece):
        line.total(piece, row_total)
        low[piece] = row_total[...].astype(BF16)
        m = lax.rem(piece - me + n, n)

        @pl.when(m > 0)
        def _():
            exchange(m).start()

    loop(0, n, finish)
    mine = pltpu.make_async_copy(low.at[me], cut.at[me], own.at[0])
    mine.start()
    line_proj.total(0, proj_grad)
    small[...] = total[...]

    def collect(m):
        along_row(m).wait_recv()
        small[...] += row_in[m]

    loop(1, n, collect)
    loop(1, group, lambda m: in_landed(m).wait_recv())
    loop(1, n, lambda m: landed(m).wait_recv())
    mine.wait()
    kept.wait()
    loop(1, group, lambda m: in_exchange(m).wait_send())
    loop(1, n, lambda m: exchange(m).wait_send())
    loop(1, n, lambda m: along_row(m).wait_send())
    loop(1, zs, lambda m: along_line(m).wait_send())
    reduce.drain()
    line.drain()
    line_proj.drain()


def back(qkv, grad_branch, proj, mixed, mixed_low, totals, marks, table, x, grad_hidden, params, mid_sums, normed,
         weight, in_cut, heads):
    cu, cl, zs = sizes()
    n = cu * cl
    rows, width = x.shape
    total_rows, cols = qkv.shape
    slab = width // (n * zs)
    block = (ITEMS, rows // ITEMS, width)
    piece = (slab, cols)
    group = in_cut.shape[0]
    input_grad, small, cut, proj_grad, in_pieces = pl.pallas_call(
        functools.partial(back_kernel, heads),
        in_specs=[*[VMEM] * 12, *[ANY] * 6],
        out_specs=[VMEM, VMEM, ANY, VMEM, ANY],
        out_shape=[
            jax.ShapeDtypeStruct(block, BF16),
            jax.ShapeDtypeStruct((8, width), F32),
            jax.ShapeDtypeStruct((n, *piece), BF16),
            jax.ShapeDtypeStruct((slab, width), F32),
            jax.ShapeDtypeStruct(in_cut.shape, BF16),
        ],
        scratch_shapes=[
            *[pltpu.VMEM((total_rows, cols // 3), F32)] * 3, pltpu.VMEM(qkv.shape, BF16),
            pltpu.VMEM(grad_branch.shape, BF16), pltpu.VMEM(proj.shape, BF16), pltpu.VMEM(mixed.shape, F32),
            pltpu.VMEM(normed.shape, BF16), pltpu.VMEM(weight.shape, BF16), pltpu.VMEM((cu, cl, *block), BF16),
            DMA((5,)), DMA((group,)), DMA((group,)),
            pltpu.VMEM((8, width), F32), pltpu.VMEM((zs, 8, width), F32), pltpu.VMEM((n, 8, width), F32),
            pltpu.VMEM((8, width), F32), pltpu.VMEM(piece, F32), DMA((zs,)), DMA((zs,)), DMA((n,)), DMA((n,)),
            DMA((n,)), DMA((n,)), DMA((2,)), pltpu.VMEM((n, *piece), BF16),
            *RowReduce.scratch(cu, rows, width), *LineReduce.scratch(zs, n, piece),
            *LineReduce.scratch(zs, 1, (slab, width)),
        ],
        cost_estimate=pl.CostEstimate(flops=0, bytes_accessed=400 << 20, transcendentals=0),
        compiler_params=pltpu.CompilerParams(collective_id=5, has_side_effects=True, vmem_limit_bytes=63 << 20),
    )(
        qkv, mixed_low, totals, *marks, table, x.reshape(block), grad_hidden.reshape(block), params, mid_sums,
        grad_branch, proj, mixed, normed, weight, in_cut,
    )
    return input_grad.reshape(rows, width), small, cut, proj_grad, in_pieces


def body(
    inputs, out_grad, doc_ids, block_pairs, qkv_weight, proj_weight, ffn_in_weight, ffn_out_weight, small_params,
    qkv_first, proj_first, ffn_in_first, ffn_out_first, small_first,
    qkv_second, proj_second, ffn_in_second, ffn_out_second, small_second,
):
    bf16 = jnp.bfloat16
    tok_rows = inputs.shape[1]
    half_rows = tok_rows // 2
    cu, cl, zs = lax.axis_size("cu"), lax.axis_size("cl"), lax.axis_size("fsdp")
    ctx_count = cu * cl
    group = cl * zs
    seq_len = tok_rows * ctx_count
    my_index = lax.axis_index(ROW)
    heads = HEADS // ctx_count
    width = heads * HEAD_DIM
    slab = qkv_weight.shape[0]
    units = ffn_out_weight.shape[0]
    hidden = units * cu
    row_in, params, qkv_low, proj_low, in_cast, pos_col, doc_col, pos_row, doc_row, table = gather_head(
        inputs[0], small_params, qkv_weight, ffn_in_weight, proj_weight, block_pairs, doc_ids
    )
    proj_low = proj_low.reshape(width, D)
    marks = (pos_col, doc_col, pos_row, doc_row)
    row_in, in_cast, out_weight_later = lax.optimization_barrier((row_in, in_cast, ffn_out_weight))
    out_low = lax.all_gather(out_weight_later.astype(bf16), "cu", axis=0, tiled=True)
    in_cut = lax.all_to_all(in_cast.reshape(group * slab, 2 * hidden), FFN_GROUP, split_axis=0, concat_axis=0, tiled=True)
    row_in = row_in.reshape(seq_len, D)
    params = params[:, :, :7, :slab].transpose(2, 0, 1, 3).reshape(7, D)
    qkv_low = qkv_low.reshape(D, 3 * width)

    bias = lax.dynamic_slice_in_dim(params[4:7], my_index * width, width, 1).reshape(1, 3 * width)
    attn_in, qkv = project(row_in, params[0:2], qkv_low, bias, table)
    mixed, mixed_low, totals, branch = attend(qkv, proj_low, marks, heads)
    branch, in_cut = lax.optimization_barrier((branch, in_cut))
    hidden_state, mlp_in, grad_all, in_low = mid_forward(
        branch, inputs[0], out_grad[0], params[2:4], in_cut.reshape(group, slab, 2 * hidden)
    )

    inner_low, grad_gate_up, grad_ffn_in = feed(mlp_in, grad_all, in_low, out_low)
    in_grad_cut = lax.psum_scatter(grad_ffn_in, "cu", scatter_dimension=0, tiled=True)

    grad_hidden, grad_branch, mid_sums, layer_out, grad_ffn_out = mid_backward(
        grad_gate_up, in_low, hidden_state, out_grad[0], params[2:4], inner_low, out_low, grad_all
    )
    layer_out = layer_out[None]
    in_grad_cut, grad_branch = lax.optimization_barrier((in_grad_cut, grad_branch))
    in_grad_cut = in_grad_cut.reshape(group, slab, 2 * hidden)
    grad_ffn_out, in_grad_cut = lax.optimization_barrier((grad_ffn_out, in_grad_cut))
    ffn_out_grad = lax.psum_scatter(grad_ffn_out, "cu", scatter_dimension=0, tiled=True)
    if seq_len <= 1024 and width % LANES == 0:
        input_grad, small_sum, qkv_grad_cut, proj_grad, in_grad = back(
            qkv, grad_branch, proj_low, mixed, mixed_low, totals, marks, table, inputs[0], grad_hidden, params[0:2],
            mid_sums, attn_in, qkv_low, in_grad_cut, heads,
        )
    else:
        grad_proj = cross_dot(mixed_low, grad_branch).astype(bf16)
        grad_joined, bias_own, in_grad = attend_back(
            qkv, grad_branch, proj_low, mixed, totals, marks, table, in_grad_cut, heads
        )
        grad_norm_part = back_dot(grad_joined, qkv_low).astype(bf16)
        grad_qkv = (
            cross_dot(attn_in, grad_joined).astype(bf16).reshape(ctx_count, zs, slab, 3 * width).transpose(1, 0, 2, 3)
        )
        bias_own = bias_own.reshape(3, width)
        grad_bias = lax.dynamic_update_slice(jnp.zeros((3, D), jnp.float32), bias_own, (0, my_index * width))
        zero_rows = jnp.zeros((2, D), jnp.float32)
        terms = jnp.concatenate([zero_rows, mid_sums, grad_bias, zero_rows[:1]], axis=0)
        input_grad, small_sum, qkv_grad_cut, proj_grad = tail(
            grad_norm_part, inputs[0], grad_hidden, params[0:2], terms, grad_qkv, grad_proj.reshape(zs, 1, slab, D)
        )
    input_grad = input_grad[None]
    my_slab = (my_index * zs + lax.axis_index("fsdp")) * slab
    small_grad = lax.dynamic_slice_in_dim(small_sum, my_slab, slab, 1)[:7]

    proj_fan = max(8 * D // seq_len, 1)
    in_new, qkv_new, out_new, proj_new = adam_all(
        (
            (ffn_in_weight, ffn_in_first, ffn_in_second, in_grad),
            (qkv_weight, qkv_first, qkv_second, qkv_grad_cut),
            (ffn_out_weight, ffn_out_first, ffn_out_second, ffn_out_grad),
            (proj_weight, proj_first, proj_second, proj_grad),
        ),
        (2.0 / math.sqrt(D), 2.0 / math.sqrt(D), 2.0 / math.sqrt(FF), 2.0 / math.sqrt(proj_fan)),
    )
    small_new = adam_update(small_params, small_first, small_second, small_grad, small_rate, 0.0)
    news = (qkv_new, proj_new, in_new, out_new, small_new)
    return (layer_out, input_grad, *(n[0] for n in news), *(n[1] for n in news), *(n[2] for n in news), small_grad)


def solution(mesh):
    ctx_count, fsdp_count = mesh.devices.shape
    fine = Mesh(mesh.devices.reshape(ctx_count // 2, 2, fsdp_count), ("cu", "cl", "fsdp"))
    tokens = P("fsdp", ROW, None)
    matrix = P(EVERY, None)
    small = P(None, EVERY)
    five = (matrix, matrix, matrix, matrix, small)
    in_specs = (tokens, tokens, P("fsdp", None), P(), *five, *five, *five)
    out_specs = (tokens, tokens, *five, *five, *five, small)
    return jax.shard_map(body, mesh=fine, in_specs=in_specs, out_specs=out_specs, check_vma=False)
```

profile of v0, /device:TPU:15, one launch (start us, length us, event | category | flops | bytes accessed | tf_op | source)
XLA Modules:
  0.0 495.3 jit_solution(2182019602157322963)
XLA Ops:
  7.2 0.0 all-gather.2.cloned.1.call-start
  7.2 0.8 copy.40.pairs
  8.0 1.0 copy-done
  9.0 1.0 copy-done.1
  10.1 0.7 copy-done.12
  10.8 0.7 copy-done.14
  11.4 76.7 %shard_map.322 = (bf16[4,2,128,2048]{3,2,1,0:T(8,128)(2,1)}, f32[8,4,8,128]{3,2,1,0:T(8,128)S(1)}, bf16[8,4,64,768]{3,2,1,0:T(8,128)(2,1)}, bf16[4,64,2048]{2,1,...) custom-call(bf16[128,2048]{1,0:T(8,128)(2,1)S(1)} %bitcast.24, ...), custom_call_target="tpu_custom_call" | custom-call | bytes 209715200 | tf_op jit(solution)/shard_map/pallas_call | solution.py:764
  88.2 0.8 copy-done.7
  89.0 1.1 convert_element_type.3
  90.1 6.9 %all-to-all-start = ((bf16[8,64,1408]{2,1,0:T(8,128)(2,1)}), bf16[8,64,1408]{2,1,0:T(8,128)(2,1)}, u32[]{:S(2)}, u32[]{:S(2)}) async-start(bf16[8,64,1408]{2,1,0:T(8,128)(2,1)} %get-tuple-element.85), calls=%async_computation | async-start | bytes 2883584 | tf_op jit(solution)/shard_map/all_to_all | solution.py:1833
  97.0 0.5 reduce-scatter.3.cloned.1.call-start
  97.6 0.1 slice.30
  97.8 0.7 slice.32.params
  98.5 0.1 slice.28.params_ref.params
  98.6 10.4 %shard_map.323 = (bf16[1024,2048]{1,0:T(8,128)(2,1)}, bf16[1024,768]{1,0:T(8,128)(2,1)S(1)}) custom-call(bf16[1024,2048]{1,0:T(8,128)(2,1)} %bitcast.41, f32[2,2048]{1,0:T(2,128)S(1)} %slice.28.params_ref.params, bf16[2048,768]{1,0:T(8,128)(2,1)} %bitcast.34, f32[1,768]{1,0:T(1,128)S(1)} %bitcast.27, f32[1024,384]{1,0:T(8,128)S(1)} %copy-done.2), custom_call_target="tpu_custom_call" | custom-call | flops 3221225472 | bytes 8388608 | tf_op jit(solution)/shard_map/pallas_call | solution.py:125
  109.1 10.3 %shard_map.324 = (f32[1024,256]{1,0:T(8,128)S(1)}, bf16[1024,256]{1,0:T(8,128)(2,1)S(1)}, f32[1024,4]{1,0:T(8,128)S(1)}, bf16[1024,2048]{1,0:T(8,128)(2,1)}) custom-call(bf16[1024,768]{1,0:T(8,128)(2,1)S(1)} %get-tuple-element.78.q_ref.qkv_ref, bf16[1024,768]{1,0:T(8,128)(2,1)S(1)} %get-tuple-element.78.q_ref.qkv_ref, bf16[256,2048]{1,0:T(8,128)(2,1)S(1)} %bitcast.25, ...), custom_call_target="tpu_custom_call" | custom-call | flops 1073741824 | bytes 16777216 | tf_op jit(solution)/shard_map/pallas_call | solution.py:168
  119.3 1.1 copy-done.3
  120.5 1.0 copy-done.5
  121.4 0.8 copy-done.9
  122.2 0.8 copy-done.10
  123.0 5.5 %all-to-all-done = bf16[8,64,1408]{2,1,0:T(8,128)(2,1)} async-done(((bf16[8,64,1408]{2,1,0:T(8,128)(2,1)}), bf16[8,64,1408]{2,1,0:T(8,128)(2,1)}, u32[]{:S(2)}, u32[]{:S(2)}) %all-to-all-start) | async-done | bytes 1441824 | tf_op jit(solution)/shard_map/all_to_all | solution.py:1833
  128.5 82.6 %shard_map.325 = (f32[4,32,2048]{2,1,0:T(8,128)}, bf16[4,2,4,32,2048]{4,3,2,1,0:T(8,128)(2,1)}, bf16[4,2,4,32,2048]{4,3,2,1,0:T(8,128)(2,1)}, bf16[4,8,64,1408]{3,2,1,0:T(8,128)(2,1)}, bf16[4,32,2048]{2,1,0:T(8,128)(2,1)}) custom-call(bf16[4,2,4,32,2048]{4,3,2,1,0:T(8,128)(2,1)} %bitcast.31, bf16[4,32,2048]{2,1,0:T(8,128)(2,1)} %bitcast.22, ...), custom_call_target="tpu_custom_call" | custom-call | bytes 209715200 | tf_op jit(solution)/shard_map/pallas_call | solution.py:1237
  211.2 26.5 %shard_map.326 = (bf16[1024,704]{1,0:T(8,128)(2,1)}, bf16[1024,1408]{1,0:T(8,128)(2,1)}, bf16[2048,1408]{1,0:T(8,128)(2,1)}) custom-call(bf16[1024,2048]{1,0:T(8,128)(2,1)} %bitcast.42, bf16[1024,2048]{1,0:T(8,128)(2,1)} %bitcast.32, bf16[2048,1408]{1,0:T(8,128)(2,1)} %bitcast.28, bf16[704,2048]{1,0:T(8,128)(2,1)} %all-gather.2.cloned.1.call-done.out_ref.weight), custom_call_target="tpu_custom_call" | custom-call | flops 14763950080 | bytes 16777216 | tf_op jit(solution)/shard_map/pallas_call | solution.py:310
  237.7 0.0 reduce-scatter.5.cloned.1.call-start
  237.7 94.2 %shard_map.327 = (f32[4,32,2048]{2,1,0:T(8,128)}, bf16[4,2,4,32,2048]{4,3,2,1,0:T(8,128)(2,1)}, f32[2,2048]{1,0:T(2,128)}, bf16[4,32,2048]{2,1,0:T(8,128)(2,1)},...) custom-call(bf16[1024,1408]{1,0:T(8,128)(2,1)} %get-tuple-element.92.back, bf16[2048,1408]{1,0:T(8,128)(2,1)} %bitcast.29, ...), custom_call_target="tpu_custom_call" | custom-call | bytes 209715200 | tf_op jit(solution)/shard_map/pallas_call | solution.py:1403
  332.0 0.0 reduce-scatter.3.cloned.1.call-done
  332.1 136.9 %shard_map.328 = (bf16[4,32,2048]{2,1,0:T(8,128)(2,1)}, f32[8,2048]{1,0:T(8,128)}, bf16[8,64,768]{2,1,0:T(8,128)(2,1)}, f32[64,2048]{1,0:T(8,128)}, bf16[8,64,1408]{2,1,0:T(8,128)(2,1)}) custom-call(bf16[1024,768]{1,0:T(8,128)(2,1)} %copy-done.3, bf16[1024,256]{1,0:T(8,128)(2,1)} %copy-done.9, f32[1024,4]{1,0:T(8,128)} %copy-done.10, s32[1024,1]{1,0:T(8,128)} %copy-done.6, ...), custom_call_target="tpu_custom_call" | custom-call | bytes 419430400 | tf_op jit(solution)/shard_map/pallas_call | solution.py:1777
  469.0 0.8 constant_dynamic-slice_fusion
  469.8 0.6 multiply_subtract_fusion
  470.4 16.5 %shard_map.329 = (f32[64,11264]{1,0:T(8,128)}, f32[64,11264]{1,0:T(8,128)}, f32[64,11264]{1,0:T(8,128)}, f32[64,6144]{1,0:T(8,128)}, f32[64,6144]{1,0:T(8,128)},...) custom-call(f32[64,11264]{1,0:T(8,128)} %refs_0_.1, ...), custom_call_target="tpu_custom_call" | custom-call | tf_op jit(solution)/shard_map/pallas_call | solution.py:417
  486.9 0.8 copy.47
  487.7 0.8 copy.48
  (48 shorter events, 0.3 us)
Async XLA Ops:
  7.2 204.0 %all-gather.2.cloned.1.call-start = ((), (), s32[]{:S(2)}) async-start(), calls=%async_computation.3 | async-start | bytes 3604480 | tf_op jit(solution)/shard_map/all_gather | solution.py:1832
  8.0 1.0 copy-start
  9.0 1.0 copy-start.1
  10.1 0.7 copy-start.12
  10.8 0.7 copy-start.14
  11.4 77.5 %copy-start.17 = (f32[176,2048]{1,0:T(8,128)S(1)}, f32[176,2048]{1,0:T(8,128)}, u32[]{:S(2)}) copy-start(f32[176,2048]{1,0:T(8,128)} %refs_8_.1) | copy-start | bytes 4325380
  88.2 0.8 copy-start.7
  89.0 20.0 %copy-start.4 = (bf16[4,64,2048]{2,1,0:T(8,128)(2,1)}, bf16[4,64,2048]{2,1,0:T(8,128)(2,1)S(1)}, u32[]{:S(2)}) copy-start(bf16[4,64,2048]{2,1,0:T(8,128)(2,1)S(1)} %get-tuple-element.79) | copy-start | bytes 3145732
  89.0 20.1 %copy-start.6 = (s32[1024,1]{1,0:T(8,128)}, s32[1024,1]{1,0:T(8,128)S(1)}, u32[]{:S(2)}) copy-start(s32[1024,1]{1,0:T(8,128)S(1)} %get-tuple-element.80.pq_ref) | copy-start | bytes 12292
  89.0 20.1 %copy-start.15 = (s32[1,1024]{1,0:T(1,128)}, s32[1,1024]{1,0:T(1,128)S(1)}, u32[]{:S(2)}) copy-start(s32[1,1024]{1,0:T(1,128)S(1)} %get-tuple-element.82.pk_ref) | copy-start | bytes 12292
  89.0 20.1 %copy-start.16 = (s32[1,1024]{1,0:T(1,128)}, s32[1,1024]{1,0:T(1,128)S(1)}, u32[]{:S(2)}) copy-start(s32[1,1024]{1,0:T(1,128)S(1)} %get-tuple-element.83.dk_ref) | copy-start | bytes 12292
  90.1 8.5 %copy-start.2 = (f32[1024,384]{1,0:T(8,128)S(1)}, f32[1024,384]{1,0:T(8,128)}, u32[]{:S(2)}) copy-start(f32[1024,384]{1,0:T(8,128)} %get-tuple-element.77.table_ref) | copy-start | bytes 4718596
  90.1 38.4 %all-to-all-start = ((bf16[8,64,1408]{2,1,0:T(8,128)(2,1)}), bf16[8,64,1408]{2,1,0:T(8,128)(2,1)}, u32[]{:S(2)}, u32[]{:S(2)}) async-start(bf16[8,64,1408]{2,1,0:T(8,128)(2,1)} %get-tuple-element.85), calls=%async_computation | async-start | bytes 2883584 | tf_op jit(solution)/shard_map/all_to_all | solution.py:1833
  97.0 235.0 %reduce-scatter.3.cloned.1.call-start = ((), (), s32[]{:S(2)}) async-start(), calls=%async_computation.4 | async-start | bytes 7208960 | tf_op jit(solution)/shard_map/reduce_scatter | solution.py:1847
  98.6 10.4 %copy-start.11 = (f32[2,2048]{1,0:T(2,128)}, f32[2,2048]{1,0:T(2,128)S(1)}, u32[]{:S(2)}) copy-start(f32[2,2048]{1,0:T(2,128)S(1)} %slice.28.params_ref.params) | copy-start | bytes 49156
  98.6 10.4 %copy-start.8 = (s32[1024,1]{1,0:T(8,128)S(1)}, s32[1024,1]{1,0:T(8,128)}, u32[]{:S(2)}) copy-start(s32[1024,1]{1,0:T(8,128)} %copy-done.7) | copy-start | bytes 12292
  119.3 1.1 copy-start.3
  120.5 1.0 copy-start.5
  121.4 0.8 copy-start.9
  122.2 0.8 copy-start.10
  237.7 232.7 %reduce-scatter.5.cloned.1.call-start = ((), (), s32[]{:S(2)}) async-start(), calls=%async_computation.5 | async-start | bytes 3604480 | tf_op jit(solution)/shard_map/reduce_scatter | solution.py:1856
  332.0 137.7 %copy-start.13 = (f32[7,64]{1,0:T(8,128)S(1)}, f32[7,64]{1,0:T(8,128)}, u32[]{:S(2)}) copy-start(f32[7,64]{1,0:T(8,128)} %small_in.1) | copy-start | bytes 5380
  332.0 137.7 %copy-start.20 = (f32[7,64]{1,0:T(8,128)S(1)}, f32[7,64]{1,0:T(8,128)}, u32[]{:S(2)}) copy-start(f32[7,64]{1,0:T(8,128)} %param.32) | copy-start | bytes 5380
  332.0 137.7 %copy-start.21 = (f32[7,64]{1,0:T(8,128)S(1)}, f32[7,64]{1,0:T(8,128)}, u32[]{:S(2)}) copy-start(f32[7,64]{1,0:T(8,128)} %param.37) | copy-start | bytes 5380
  470.4 16.5 %copy-start.18 = (bf16[4,32,2048]{2,1,0:T(8,128)(2,1)S(1)}, bf16[4,32,2048]{2,1,0:T(8,128)(2,1)}, u32[]{:S(2)}) copy-start(bf16[4,32,2048]{2,1,0:T(8,128)(2,1)} %get-tuple-element.95) | copy-start | bytes 1572868
  470.4 17.3 %copy-start.19 = (bf16[4,32,2048]{2,1,0:T(8,128)(2,1)S(1)}, bf16[4,32,2048]{2,1,0:T(8,128)(2,1)}, u32[]{:S(2)}) copy-start(bf16[4,32,2048]{2,1,0:T(8,128)(2,1)} %get-tuple-element.108) | copy-start | bytes 1572868
Sparse Core Ops, SparseCore 0:
  90.2 42.3 all-gather.1
  237.8 85.1 reduce-scatter.2
  332.1 43.9 reduce-scatter.4
where the time goes:
time: 499 us; the launch traced here: 495 us
  Pallas kernels  454 us (91%)
  between operations  14.3 us (3%)
  local copies, waits for them, and re-layouts  12.1 us (2%)
  starting transfers between devices  7.48 us (1%)
  waiting for transfers between devices  5.61 us (1%)
    pallas_call x1, Pallas kernels, back(): pl.pallas_call(functools.partial(back_kernel, heads), in_specs=[*[VMEM] *...  137 us
    pallas_call x1, Pallas kernels, mid_backward(): pl.pallas_call(mid_backward_kernel, in_specs=[ANY, ANY, VMEM, VMEM, VMEM,...  94.2 us
    pallas_call x1, Pallas kernels, mid_forward(): pl.pallas_call(mid_forward_kernel, in_specs=[ANY, VMEM, VMEM, VMEM, ANY],...  82.6 us
    pallas_call x1, Pallas kernels, gather_head(): pl.pallas_call(head_kernel, in_specs=[ANY, VMEM, ANY, ANY, ANY, pl.BlockS...  76.7 us
    pallas_call x1, Pallas kernels, feed(): pl.pallas_call(feed_kernel, grid=(rows // block,), in_specs=[by_row(width...  26.5 us
    pallas_call x1, Pallas kernels, adam_all(): pl.pallas_call(functools.partial(adam_kernel, rates, chunks), in_specs=[a...  16.5 us
    pallas_call x1, Pallas kernels, project(): pl.pallas_call(project_kernel, grid=(rows // block,), in_specs=[by_row(wi...  10.4 us
    unnamed x49, local copies, waits for them, and re-layouts  10.4 us
  transfers between devices with their start and end apart: 4, of which 1 were waited for; matrix products, arithmetic and copies ran while one was open for 0% of the time, Pallas kernels for 68%

commit v1 on v0

--- a/solution.py
+++ b/solution.py
@@ -1199,13 +1199,13 @@
     reduce.merge()
     for item in range(ITEMS):
         reduce.send(item, 0)
-    plane.start()
     for item in range(ITEMS):
         gather_grads.forward(item, 1)
     for phase in range(1, reduce.phases):
         for item in range(ITEMS):
             reduce.add(item, phase - 1)
             reduce.send(item, phase)
+    plane.start()
     for step in range(2, gather.count - 1):
         for item in range(ITEMS):
             gather_grads.forward(item, step)

time: 499 us -> 500 us (level)
  no operation moved by 1% of the time
where the time goes in v1:
time: 500 us; the launch traced here: 497 us
  Pallas kernels  456 us (91%)
  between operations  14.3 us (3%)
  local copies, waits for them, and re-layouts  12.1 us (2%)
  starting transfers between devices  7.48 us (1%)
  waiting for transfers between devices  5.61 us (1%)
    pallas_call x1, Pallas kernels, back(): pl.pallas_call(functools.partial(back_kernel, heads), in_specs=[*[VMEM] *...  139 us
    pallas_call x1, Pallas kernels, mid_backward(): pl.pallas_call(mid_backward_kernel, in_specs=[ANY, ANY, VMEM, VMEM, VMEM,...  96.2 us
    pallas_call x1, Pallas kernels, mid_forward(): pl.pallas_call(mid_forward_kernel, in_specs=[ANY, VMEM, VMEM, VMEM, ANY],...  80.3 us
    pallas_call x1, Pallas kernels, gather_head(): pl.pallas_call(head_kernel, in_specs=[ANY, VMEM, ANY, ANY, ANY, pl.BlockS...  76.7 us
    pallas_call x1, Pallas kernels, feed(): pl.pallas_call(feed_kernel, grid=(rows // block,), in_specs=[by_row(width...  26.5 us
    pallas_call x1, Pallas kernels, adam_all(): pl.pallas_call(functools.partial(adam_kernel, rates, chunks), in_specs=[a...  16.5 us
    pallas_call x1, Pallas kernels, project(): pl.pallas_call(project_kernel, grid=(rows // block,), in_specs=[by_row(wi...  10.4 us
    unnamed x49, local copies, waits for them, and re-layouts  10.4 us
  transfers between devices with their start and end apart: 4, of which 1 were waited for; matrix products, arithmetic and copies ran while one was open for 0% of the time, Pallas kernels for 68%

profile of v1, /device:TPU:15, one launch (start us, length us, event | category | flops | bytes accessed | tf_op | source)
XLA Modules:
  0.0 496.7 jit_solution(10246874156371358022)
XLA Ops:
  7.2 0.0 all-gather.2.cloned.1.call-start
  7.2 0.8 copy.40.pairs
  8.0 1.0 copy-done
  9.0 1.0 copy-done.1
  10.1 0.7 copy-done.12
  10.8 0.7 copy-done.14
  11.4 76.7 %shard_map.322 = (bf16[4,2,128,2048]{3,2,1,0:T(8,128)(2,1)}, f32[8,4,8,128]{3,2,1,0:T(8,128)S(1)}, bf16[8,4,64,768]{3,2,1,0:T(8,128)(2,1)}, bf16[4,64,2048]{2,1,...) custom-call(bf16[128,2048]{1,0:T(8,128)(2,1)S(1)} %bitcast.24, ...), custom_call_target="tpu_custom_call" | custom-call | bytes 209715200 | tf_op jit(solution)/shard_map/pallas_call | solution.py:764
  88.2 0.8 copy-done.7
  89.0 1.1 convert_element_type.3
  90.1 6.9 %all-to-all-start = ((bf16[8,64,1408]{2,1,0:T(8,128)(2,1)}), bf16[8,64,1408]{2,1,0:T(8,128)(2,1)}, u32[]{:S(2)}, u32[]{:S(2)}) async-start(bf16[8,64,1408]{2,1,0:T(8,128)(2,1)} %get-tuple-element.85), calls=%async_computation | async-start | bytes 2883584 | tf_op jit(solution)/shard_map/all_to_all | solution.py:1833
  97.0 0.5 reduce-scatter.3.cloned.1.call-start
  97.6 0.1 slice.30
  97.8 0.7 slice.32.params
  98.5 0.1 slice.28.params_ref.params
  98.6 10.4 %shard_map.323 = (bf16[1024,2048]{1,0:T(8,128)(2,1)}, bf16[1024,768]{1,0:T(8,128)(2,1)S(1)}) custom-call(bf16[1024,2048]{1,0:T(8,128)(2,1)} %bitcast.41, f32[2,2048]{1,0:T(2,128)S(1)} %slice.28.params_ref.params, bf16[2048,768]{1,0:T(8,128)(2,1)} %bitcast.34, f32[1,768]{1,0:T(1,128)S(1)} %bitcast.27, f32[1024,384]{1,0:T(8,128)S(1)} %copy-done.2), custom_call_target="tpu_custom_call" | custom-call | flops 3221225472 | bytes 8388608 | tf_op jit(solution)/shard_map/pallas_call | solution.py:125
  109.1 10.3 %shard_map.324 = (f32[1024,256]{1,0:T(8,128)S(1)}, bf16[1024,256]{1,0:T(8,128)(2,1)S(1)}, f32[1024,4]{1,0:T(8,128)S(1)}, bf16[1024,2048]{1,0:T(8,128)(2,1)}) custom-call(bf16[1024,768]{1,0:T(8,128)(2,1)S(1)} %get-tuple-element.78.q_ref.qkv_ref, bf16[1024,768]{1,0:T(8,128)(2,1)S(1)} %get-tuple-element.78.q_ref.qkv_ref, bf16[256,2048]{1,0:T(8,128)(2,1)S(1)} %bitcast.25, ...), custom_call_target="tpu_custom_call" | custom-call | flops 1073741824 | bytes 16777216 | tf_op jit(solution)/shard_map/pallas_call | solution.py:168
  119.3 1.1 copy-done.3
  120.5 1.0 copy-done.5
  121.4 0.8 copy-done.9
  122.2 0.8 copy-done.10
  123.0 5.5 %all-to-all-done = bf16[8,64,1408]{2,1,0:T(8,128)(2,1)} async-done(((bf16[8,64,1408]{2,1,0:T(8,128)(2,1)}), bf16[8,64,1408]{2,1,0:T(8,128)(2,1)}, u32[]{:S(2)}, u32[]{:S(2)}) %all-to-all-start) | async-done | bytes 1441824 | tf_op jit(solution)/shard_map/all_to_all | solution.py:1833
  128.5 80.3 %shard_map.325 = (f32[4,32,2048]{2,1,0:T(8,128)}, bf16[4,2,4,32,2048]{4,3,2,1,0:T(8,128)(2,1)}, bf16[4,2,4,32,2048]{4,3,2,1,0:T(8,128)(2,1)}, bf16[4,8,64,1408]{3,2,1,0:T(8,128)(2,1)}, bf16[4,32,2048]{2,1,0:T(8,128)(2,1)}) custom-call(bf16[4,2,4,32,2048]{4,3,2,1,0:T(8,128)(2,1)} %bitcast.31, bf16[4,32,2048]{2,1,0:T(8,128)(2,1)} %bitcast.22, ...), custom_call_target="tpu_custom_call" | custom-call | bytes 209715200 | tf_op jit(solution)/shard_map/pallas_call | solution.py:1237
  208.9 0.0 all-gather.2.cloned.1.call-done.out_ref.weight
  208.9 26.5 %shard_map.326 = (bf16[1024,704]{1,0:T(8,128)(2,1)}, bf16[1024,1408]{1,0:T(8,128)(2,1)}, bf16[2048,1408]{1,0:T(8,128)(2,1)}) custom-call(bf16[1024,2048]{1,0:T(8,128)(2,1)} %bitcast.42, bf16[1024,2048]{1,0:T(8,128)(2,1)} %bitcast.32, bf16[2048,1408]{1,0:T(8,128)(2,1)} %bitcast.28, bf16[704,2048]{1,0:T(8,128)(2,1)} %all-gather.2.cloned.1.call-done.out_ref.weight), custom_call_target="tpu_custom_call" | custom-call | flops 14763950080 | bytes 16777216 | tf_op jit(solution)/shard_map/pallas_call | solution.py:310
  235.4 0.0 reduce-scatter.5.cloned.1.call-start
  235.5 96.2 %shard_map.327 = (f32[4,32,2048]{2,1,0:T(8,128)}, bf16[4,2,4,32,2048]{4,3,2,1,0:T(8,128)(2,1)}, f32[2,2048]{1,0:T(2,128)}, bf16[4,32,2048]{2,1,0:T(8,128)(2,1)},...) custom-call(bf16[1024,1408]{1,0:T(8,128)(2,1)} %get-tuple-element.92.back, bf16[2048,1408]{1,0:T(8,128)(2,1)} %bitcast.29, ...), custom_call_target="tpu_custom_call" | custom-call | bytes 209715200 | tf_op jit(solution)/shard_map/pallas_call | solution.py:1403
  331.7 138.7 %shard_map.328 = (bf16[4,32,2048]{2,1,0:T(8,128)(2,1)}, f32[8,2048]{1,0:T(8,128)}, bf16[8,64,768]{2,1,0:T(8,128)(2,1)}, f32[64,2048]{1,0:T(8,128)}, bf16[8,64,1408]{2,1,0:T(8,128)(2,1)}) custom-call(bf16[1024,768]{1,0:T(8,128)(2,1)} %copy-done.3, bf16[1024,256]{1,0:T(8,128)(2,1)} %copy-done.9, f32[1024,4]{1,0:T(8,128)} %copy-done.10, s32[1024,1]{1,0:T(8,128)} %copy-done.6, ...), custom_call_target="tpu_custom_call" | custom-call | bytes 419430400 | tf_op jit(solution)/shard_map/pallas_call | solution.py:1777
  470.4 0.8 constant_dynamic-slice_fusion
  471.2 0.6 multiply_subtract_fusion
  471.8 16.5 %shard_map.329 = (f32[64,11264]{1,0:T(8,128)}, f32[64,11264]{1,0:T(8,128)}, f32[64,11264]{1,0:T(8,128)}, f32[64,6144]{1,0:T(8,128)}, f32[64,6144]{1,0:T(8,128)},...) custom-call(f32[64,11264]{1,0:T(8,128)} %refs_0_.1, ...), custom_call_target="tpu_custom_call" | custom-call | tf_op jit(solution)/shard_map/pallas_call | solution.py:417
  488.3 0.8 copy.47
  489.1 0.8 copy.48
  (48 shorter events, 0.3 us)
Async XLA Ops:
  7.2 201.7 %all-gather.2.cloned.1.call-start = ((), (), s32[]{:S(2)}) async-start(), calls=%async_computation.3 | async-start | bytes 3604480 | tf_op jit(solution)/shard_map/all_gather | solution.py:1832
  8.0 1.0 copy-start
  9.0 1.0 copy-start.1
  10.1 0.7 copy-start.12
  10.8 0.7 copy-start.14
  11.4 77.5 %copy-start.17 = (f32[176,2048]{1,0:T(8,128)S(1)}, f32[176,2048]{1,0:T(8,128)}, u32[]{:S(2)}) copy-start(f32[176,2048]{1,0:T(8,128)} %refs_8_.1) | copy-start | bytes 4325380
  88.2 0.8 copy-start.7
  89.0 20.0 %copy-start.4 = (bf16[4,64,2048]{2,1,0:T(8,128)(2,1)}, bf16[4,64,2048]{2,1,0:T(8,128)(2,1)S(1)}, u32[]{:S(2)}) copy-start(bf16[4,64,2048]{2,1,0:T(8,128)(2,1)S(1)} %get-tuple-element.79) | copy-start | bytes 3145732
  89.0 20.1 %copy-start.6 = (s32[1024,1]{1,0:T(8,128)}, s32[1024,1]{1,0:T(8,128)S(1)}, u32[]{:S(2)}) copy-start(s32[1024,1]{1,0:T(8,128)S(1)} %get-tuple-element.80.pq_ref) | copy-start | bytes 12292
  89.0 20.1 %copy-start.15 = (s32[1,1024]{1,0:T(1,128)}, s32[1,1024]{1,0:T(1,128)S(1)}, u32[]{:S(2)}) copy-start(s32[1,1024]{1,0:T(1,128)S(1)} %get-tuple-element.82.pk_ref) | copy-start | bytes 12292
  89.0 20.1 %copy-start.16 = (s32[1,1024]{1,0:T(1,128)}, s32[1,1024]{1,0:T(1,128)S(1)}, u32[]{:S(2)}) copy-start(s32[1,1024]{1,0:T(1,128)S(1)} %get-tuple-element.83.dk_ref) | copy-start | bytes 12292
  90.1 8.5 %copy-start.2 = (f32[1024,384]{1,0:T(8,128)S(1)}, f32[1024,384]{1,0:T(8,128)}, u32[]{:S(2)}) copy-start(f32[1024,384]{1,0:T(8,128)} %get-tuple-element.77.table_ref) | copy-start | bytes 4718596
  90.1 38.4 %all-to-all-start = ((bf16[8,64,1408]{2,1,0:T(8,128)(2,1)}), bf16[8,64,1408]{2,1,0:T(8,128)(2,1)}, u32[]{:S(2)}, u32[]{:S(2)}) async-start(bf16[8,64,1408]{2,1,0:T(8,128)(2,1)} %get-tuple-element.85), calls=%async_computation | async-start | bytes 2883584 | tf_op jit(solution)/shard_map/all_to_all | solution.py:1833
  97.0 234.6 %reduce-scatter.3.cloned.1.call-start = ((), (), s32[]{:S(2)}) async-start(), calls=%async_computation.4 | async-start | bytes 7208960 | tf_op jit(solution)/shard_map/reduce_scatter | solution.py:1847
  98.6 10.4 %copy-start.11 = (f32[2,2048]{1,0:T(2,128)}, f32[2,2048]{1,0:T(2,128)S(1)}, u32[]{:S(2)}) copy-start(f32[2,2048]{1,0:T(2,128)S(1)} %slice.28.params_ref.params) | copy-start | bytes 49156
  98.6 10.4 %copy-start.8 = (s32[1024,1]{1,0:T(8,128)S(1)}, s32[1024,1]{1,0:T(8,128)}, u32[]{:S(2)}) copy-start(s32[1024,1]{1,0:T(8,128)} %copy-done.7) | copy-start | bytes 12292
  119.3 1.1 copy-start.3
  120.5 1.0 copy-start.5
  121.4 0.8 copy-start.9
  122.2 0.8 copy-start.10
  235.4 236.4 %reduce-scatter.5.cloned.1.call-start = ((), (), s32[]{:S(2)}) async-start(), calls=%async_computation.5 | async-start | bytes 3604480 | tf_op jit(solution)/shard_map/reduce_scatter | solution.py:1856
  331.7 139.5 %copy-start.13 = (f32[7,64]{1,0:T(8,128)S(1)}, f32[7,64]{1,0:T(8,128)}, u32[]{:S(2)}) copy-start(f32[7,64]{1,0:T(8,128)} %small_in.1) | copy-start | bytes 5380
  331.7 139.5 %copy-start.20 = (f32[7,64]{1,0:T(8,128)S(1)}, f32[7,64]{1,0:T(8,128)}, u32[]{:S(2)}) copy-start(f32[7,64]{1,0:T(8,128)} %param.32) | copy-start | bytes 5380
  331.7 139.5 %copy-start.21 = (f32[7,64]{1,0:T(8,128)S(1)}, f32[7,64]{1,0:T(8,128)}, u32[]{:S(2)}) copy-start(f32[7,64]{1,0:T(8,128)} %param.37) | copy-start | bytes 5380
  471.8 16.5 %copy-start.18 = (bf16[4,32,2048]{2,1,0:T(8,128)(2,1)S(1)}, bf16[4,32,2048]{2,1,0:T(8,128)(2,1)}, u32[]{:S(2)}) copy-start(bf16[4,32,2048]{2,1,0:T(8,128)(2,1)} %get-tuple-element.95) | copy-start | bytes 1572868
  471.8 17.3 %copy-start.19 = (bf16[4,32,2048]{2,1,0:T(8,128)(2,1)S(1)}, bf16[4,32,2048]{2,1,0:T(8,128)(2,1)}, u32[]{:S(2)}) copy-start(bf16[4,32,2048]{2,1,0:T(8,128)(2,1)} %get-tuple-element.108) | copy-start | bytes 1572868
Sparse Core Ops, SparseCore 0:
  90.2 42.3 all-gather.1
  235.5 85.6 reduce-scatter.2
  331.8 45.1 reduce-scatter.4
